TPU v7x, 256 devices: a whole 4x4x8 slice. The times are simulated.
256 devices in a mesh: section: 8 (over x, core), node: 4 (over z_lo), local: 8 (over z_hi, y).
Axes of the slice: x: 4, y: 4, z: 8 (z_hi: 2, z_lo: 4; z = z_hi * 4 + z_lo), core: 2. Of those that a mesh axis runs over, the one named last changes fastest.
Arguments:
- x_fwd: bfloat16 [8, 2048, 3584], P('section', ('node', 'local')), may hold values from -6 to 6
- route_fwd: int32 [8, 2048, 2], P('section', ('node', 'local')), may hold values from 0 to 3, all different within a row; in each aligned block of 64 rows (0 to 63, 64 to 127, ..., all dimensions but the last counted through in order) at most 36 rows name the same one
- weight_fwd: float32 [8, 2048, 2], P('section', ('node', 'local')), may hold values from 0.2 to 1.2
- x_bwd: bfloat16 [8, 2048, 3584], P('section', ('node', 'local')), may hold values from -6 to 6
- grad_out: bfloat16 [8, 2048, 3584], P('section', ('node', 'local')), may hold values from -6 to 6
- route_bwd: int32 [8, 2048, 2], P('section', ('node', 'local')), may hold values from 0 to 3, all different within a row; in each aligned block of 64 rows (0 to 63, 64 to 127, ..., all dimensions but the last counted through in order) at most 36 rows name the same one
- weight_bwd: float32 [8, 2048, 2], P('section', ('node', 'local')), may hold values from 0.2 to 1.2
- saved_pre: bfloat16 [8, 4, 1152, 2, 2048], P('section', 'node', None, None, 'local'), may hold values from -6 to 6
- norm_gain: float32 [8, 3584], P('section'), may hold values from 0.5 to 1.5
- w_gate: bfloat16 [8, 4, 3584, 2048], P('section', 'node', None, 'local'), may hold values from -0.09375 to 0.09375
- w_up: bfloat16 [8, 4, 3584, 2048], P('section', 'node', None, 'local'), may hold values from -0.09375 to 0.09375
- w_down: bfloat16 [8, 4, 2048, 3584], P('section', 'node', 'local'), may hold values from -0.125 to 0.125
Outputs:
- act_next: bfloat16 [8, 2048, 3584], P('section', ('node', 'local'))
- grad_prev: bfloat16 [8, 2048, 3584], P('section', ('node', 'local'))
Inputs may be any that keep to these rules, and one draw needn't show every extreme that they name: `route_fwd`: each row names 2 different experts. Among the 64 rows of one device no expert is named more than 36 times, and in every draw some device names some expert exactly 36 times. `route_bwd`: each row names 2 different experts. Among the 64 rows of one device no expert is named more than 36 times, and in every draw some device names some expert exactly 36 times.
All inputs are finite; a program needn't handle non-finite values.
Results may differ from a plain program's by a relative error of at most 0.01.
Values may be sent and summed in bfloat16 or wider, within the bound.
No kernel may reach another device: no remote copies, remote signals or barrier semaphores. Data moves between devices by JAX's collectives and lax.ppermute only.
A program may use at most 128 MiB of HBM per device.

v0:
```python
import jax
import jax.numpy as jnp
from jax import lax
from jax.sharding import PartitionSpec as P

EPSILON = 1e-06


def passed_along(shard, axis, by):
    size = lax.axis_size(axis)
    return lax.ppermute(shard, axis, [(i, (i + by) % size) for i in range(size)])


def rms_scale(values):
    return lax.rsqrt(jnp.mean(values * values, axis=-1, keepdims=True) + EPSILON)


def slot_index(route, experts, capacity):
    choose = (route[:, :, None] == jnp.arange(experts, dtype=jnp.int32)[None, None, :]).astype(
        jnp.int32
    )
    per_token = jnp.sum(choose, axis=1)
    earlier = jnp.cumsum(per_token, axis=0) - per_token
    slot = jnp.sum(choose * earlier[:, None, :], axis=2)
    return route * capacity + slot


def place_rows(source, target, total):
    hits = target[None, :, :] == jnp.arange(total, dtype=jnp.int32)[:, None, None]
    table = jnp.sum(hits.astype(jnp.int32), axis=2).astype(jnp.bfloat16)
    return jnp.dot(table, source, preferred_element_type=jnp.float32).astype(jnp.bfloat16)


def return_flat(block):
    return lax.all_to_all(block, ("node", "local"), split_axis=0, concat_axis=0, tiled=True)


def local(
    x_fwd,
    route_fwd,
    weight_fwd,
    x_bwd,
    grad_out,
    route_bwd,
    weight_bwd,
    saved_pre,
    norm_gain,
    w_gate,
    w_up,
    w_down,
):
    experts = lax.axis_size("node")
    shard_count = lax.axis_size("local")
    tokens_here = x_fwd.shape[1]
    feature_width = x_fwd.shape[2]
    slot_total = saved_pre.shape[2]
    capacity = slot_total // (experts * shard_count)
    shard_units = w_gate.shape[3]
    gate_w = w_gate[0, 0]
    up_w = w_up[0, 0]
    down_w = w_down[0, 0]
    stored = saved_pre[0, 0]
    gain = norm_gain[0]
    contract_last = (((1,), (1,)), ((), ()))
    x_first = x_fwd[0].astype(jnp.float32)
    normed = (x_first * rms_scale(x_first) * gain).astype(jnp.bfloat16)
    rows_first = slot_index(route_fwd[0], experts, capacity)
    send_first = place_rows(normed, rows_first, experts * capacity)
    x_second = x_bwd[0].astype(jnp.float32)
    scale_second = rms_scale(x_second)
    upstream = grad_out[0]
    scaled = (weight_bwd[0][:, :, None] * upstream[:, None, :].astype(jnp.float32)).astype(
        jnp.bfloat16
    )
    rows_second = slot_index(route_bwd[0], experts, capacity)
    send_second = place_rows(
        scaled.reshape(-1, feature_width), rows_second.reshape(-1, 1), experts * capacity
    )
    wide_first = jnp.broadcast_to(
        send_first.reshape(experts, 1, capacity, feature_width),
        (experts, shard_count, capacity, feature_width),
    ).reshape(experts * shard_count, capacity, feature_width)
    wide_second = jnp.broadcast_to(
        send_second.reshape(experts, 1, capacity, feature_width),
        (experts, shard_count, capacity, feature_width),
    ).reshape(experts * shard_count, capacity, feature_width)
    got_first, got_second = (
        lax.all_to_all(wide_first, ("node", "local"), split_axis=0, concat_axis=0, tiled=True),
        lax.all_to_all(wide_second, ("node", "local"), split_axis=0, concat_axis=0, tiled=True),
    )
    arrived_first = got_first.reshape(slot_total, feature_width)
    arrived_second = got_second.reshape(slot_total, feature_width)
    gate = jnp.dot(arrived_first, gate_w, preferred_element_type=jnp.float32)
    upper = jnp.dot(arrived_first, up_w, preferred_element_type=jnp.float32)
    hidden = (jax.nn.silu(gate) * upper).astype(jnp.bfloat16)
    partial_value = jnp.dot(hidden, down_w, preferred_element_type=jnp.float32).astype(jnp.bfloat16)
    came_back = return_flat(partial_value.reshape(experts * shard_count, capacity, feature_width))
    out_first = (
        jnp.sum(
            came_back.reshape(experts, shard_count, capacity, feature_width).astype(jnp.float32),
            axis=1,
        )
        .astype(jnp.bfloat16)
        .reshape(experts * capacity, feature_width)
    )
    picked = (
        jnp.take(out_first, rows_first.reshape(-1), axis=0)
        .reshape(tokens_here, -1, feature_width)
        .astype(jnp.float32)
    )
    layer_out = (x_first + jnp.sum(weight_fwd[0][:, :, None] * picked, axis=1)).astype(jnp.bfloat16)
    act_next = passed_along(layer_out, "section", 1)
    ordered = (
        stored.reshape(shard_count, experts, capacity, 2, shard_units)
        .transpose(1, 0, 2, 3, 4)
        .reshape(slot_total, 2, shard_units)
    )
    hidden_grad = lax.dot_general(
        arrived_second, down_w, contract_last, preferred_element_type=jnp.float32
    )
    gate = ordered[:, 0, :].astype(jnp.float32)
    upper = ordered[:, 1, :].astype(jnp.float32)
    sigma = jax.nn.sigmoid(gate)
    grad_gate = hidden_grad * upper * sigma * (1.0 + gate * (1.0 - sigma))
    grad_upper = hidden_grad * gate * sigma
    grads_pre = jnp.stack([grad_gate, grad_upper], axis=1).astype(jnp.bfloat16)
    from_gate = lax.dot_general(
        grads_pre[:, 0, :], gate_w, contract_last, preferred_element_type=jnp.float32
    )
    from_upper = lax.dot_general(
        grads_pre[:, 1, :], up_w, contract_last, preferred_element_type=jnp.float32
    )
    partial_back = (from_gate + from_upper).astype(jnp.bfloat16)
    came_back = return_flat(partial_back.reshape(experts * shard_count, capacity, feature_width))
    out_second = (
        jnp.sum(
            came_back.reshape(experts, shard_count, capacity, feature_width).astype(jnp.float32),
            axis=1,
        )
        .astype(jnp.bfloat16)
        .reshape(experts * capacity, feature_width)
    )
    picked_back = (
        jnp.take(out_second, rows_second.reshape(-1), axis=0)
        .reshape(tokens_here, -1, feature_width)
        .astype(jnp.float32)
    )
    normed_grad = jnp.sum(picked_back, axis=1)
    along = gain * normed_grad
    cubed = scale_second * scale_second * scale_second
    input_grad = (
        upstream.astype(jnp.float32)
        + scale_second * along
        - x_second * cubed * jnp.mean(along * x_second, axis=-1, keepdims=True)
    )
    input_grad = input_grad.astype(jnp.bfloat16)
    grad_prev = passed_along(input_grad, "section", -1)
    return (act_next[None], grad_prev[None])


def solution(mesh):
    in_specs = (
        P("section", ("node", "local"), None),
        P("section", ("node", "local"), None),
        P("section", ("node", "local"), None),
        P("section", ("node", "local"), None),
        P("section", ("node", "local"), None),
        P("section", ("node", "local"), None),
        P("section", ("node", "local"), None),
        P("section", "node", None, None, "local"),
        P("section", None),
        P("section", "node", None, "local"),
        P("section", "node", None, "local"),
        P("section", "node", "local", None),
    )
    out_specs = (P("section", ("node", "local"), None), P("section", ("node", "local"), None))
    return jax.shard_map(local, mesh=mesh, in_specs=in_specs, out_specs=out_specs, check_vma=False)
```

profile of v0, /device:TPU:1, one launch (start us, length us, event | category | flops | bytes accessed | tf_op | source)
XLA Modules:
  0.0 936.3 jit_solution(6459690575637920762)
XLA Ops:
  0.6 0.8 broadcast_multiply_fusion
  3.6 2.0 bitcast_convert_fusion
  5.6 0.8 copy.45
  6.4 1.9 multiply_convert_fusion
  8.3 1.3 convert_element_type.160
  9.6 2.6 convolution_convert_fusion.1
  12.2 1.3 broadcast_in_dim.42
  13.5 4.2 broadcast_in_dim.43
  17.7 12.3 %all-to-all-start.2 = ((bf16[32,36,3584]{2,1,0:T(8,128)(2,1)}), bf16[32,36,3584]{2,1,0:T(8,128)(2,1)}, u32[]{:S(2)}, u32[]{:S(2)}) async-start(bf16[32,36,3584]{2,1,0:T(8,128)(2,1)} %bitcast.79), calls=%async_computation.2 | async-start | bytes 18350080 | tf_op jit(solution)/shard_map/all_to_all | solution.py:89
  30.7 1.5 convolution_convert_fusion.2
  32.1 1.3 broadcast_in_dim.21
  33.5 204.1 %all-to-all-done.2 = bf16[32,36,3584]{2,1,0:T(8,128)(2,1)} async-done(((bf16[32,36,3584]{2,1,0:T(8,128)(2,1)}), bf16[32,36,3584]{2,1,0:T(8,128)(2,1)}, u32[]{:S(2)}, u32[]{:S(2)}) %all-to-all-start.2) | async-done | bytes 8257568 | tf_op jit(solution)/shard_map/all_to_all | solution.py:89
  237.5 4.2 broadcast_in_dim.22
  241.7 15.9 %all-to-all-start = ((bf16[32,36,3584]{2,1,0:T(8,128)(2,1)}), bf16[32,36,3584]{2,1,0:T(8,128)(2,1)}, u32[]{:S(2)}, u32[]{:S(2)}) async-start(bf16[32,36,3584]{2,1,0:T(8,128)(2,1)} %bitcast.80), calls=%async_computation | async-start | bytes 18350080 | tf_op jit(solution)/shard_map/all_to_all | solution.py:88
  257.7 0.8 copy.46
  258.5 2.5 fusion.53
  261.0 12.6 %reshape.231 = bf16[1152,3584]{1,0:T(8,128)(2,1)} reshape(bf16[32,36,3584]{2,1,0:T(8,128)(2,1)} %all-to-all-done.2) | data formatting | bytes 16515072 | tf_op jit(solution)/shard_map/reshape | solution.py:92
  273.6 6.3 fusion.2
  279.9 8.3 fusion.7
  288.3 11.5 %fusion = bf16[1152,3584]{1,0:T(8,128)(2,1)} fusion(f32[1152,3584]{1,0:T(8,128)} %fusion.7, bf16[1,1,3584,256]{3,2,1,0:T(8,128)(2,1)S(1)} %copy-done, f32[1152,256]{1,0:T(8,128)S(1)} %fusion.2, bf16[1152,1,256]{2,1,0:T(2,128)(2,1)S(1)} %get-tuple-element.9), kind=kOutput, calls=%fused_computation.3 | convolution fusion | flops 2124251136 | bytes 28377088 | tf_op jit(solution)/shard_map/dot_general | solution.py:130
  299.7 12.6 %reshape.233 = bf16[32,36,3584]{2,1,0:T(8,128)(2,1)} reshape(bf16[1152,3584]{1,0:T(8,128)(2,1)} %fusion) | data formatting | bytes 16515072 | tf_op jit(solution)/shard_map/reshape | solution.py:134
  312.3 151.3 %all-to-all-done = bf16[32,36,3584]{2,1,0:T(8,128)(2,1)} async-done(((bf16[32,36,3584]{2,1,0:T(8,128)(2,1)}), bf16[32,36,3584]{2,1,0:T(8,128)(2,1)}, u32[]{:S(2)}, u32[]{:S(2)}) %all-to-all-start) | async-done | bytes 8257568 | tf_op jit(solution)/shard_map/all_to_all | solution.py:88
  463.6 15.3 %all-to-all-start.3 = ((bf16[32,36,3584]{2,1,0:T(8,128)(2,1)}), bf16[32,36,3584]{2,1,0:T(8,128)(2,1)}, u32[]{:S(2)}, u32[]{:S(2)}) async-start(bf16[32,36,3584]{2,1,0:T(8,128)(2,1)} %reshape.233), calls=%async_computation.3 | async-start | bytes 18350080 | tf_op jit(solution)/shard_map/all_to_all | solution.py:35
  478.9 12.6 %reshape.226 = bf16[1152,3584]{1,0:T(8,128)(2,1)} reshape(bf16[32,36,3584]{2,1,0:T(8,128)(2,1)} %all-to-all-done) | data formatting | bytes 16515072 | tf_op jit(solution)/shard_map/reshape | solution.py:91
  491.4 6.1 fusion.9
  497.6 13.5 %convolution_convert_fusion = bf16[1152,3584]{1,0:T(8,128)(2,1)} fusion(bf16[1,1,256,3584]{3,2,1,0:T(8,128)(2,1)} %param.25, bf16[1152,3584]{1,0:T(8,128)(2,1)} %reshape.226, bf16[1,1,3584,256]{3,2,1,0:T(8,128)(2,1)S(1)} %copy-done, f32[1152,256]{1,0:T(8,128)S(1)} %fusion.9), kind=kOutput, calls=%fused_computation.4 | convolution fusion | flops 4233756672 | bytes 21364736 | tf_op jit(solution)/shard_map/dot_general | solution.py:96
  511.1 12.5 %reshape.227 = bf16[32,36,3584]{2,1,0:T(8,128)(2,1)} reshape(bf16[1152,3584]{1,0:T(8,128)(2,1)} %convolution_convert_fusion) | data formatting | bytes 16515072 | tf_op jit(solution)/shard_map/reshape | solution.py:97
  523.7 161.6 %all-to-all-done.3 = bf16[32,36,3584]{2,1,0:T(8,128)(2,1)} async-done(((bf16[32,36,3584]{2,1,0:T(8,128)(2,1)}), bf16[32,36,3584]{2,1,0:T(8,128)(2,1)}, u32[]{:S(2)}, u32[]{:S(2)}) %all-to-all-start.3) | async-done | bytes 8257568 | tf_op jit(solution)/shard_map/all_to_all | solution.py:35
  685.3 14.8 %all-to-all-start.1 = ((bf16[32,36,3584]{2,1,0:T(8,128)(2,1)}), bf16[32,36,3584]{2,1,0:T(8,128)(2,1)}, u32[]{:S(2)}, u32[]{:S(2)}) async-start(bf16[32,36,3584]{2,1,0:T(8,128)(2,1)} %reshape.227), calls=%async_computation.1 | async-start | bytes 18350080 | tf_op jit(solution)/shard_map/all_to_all | solution.py:35
  700.7 6.3 bitcast_reduce_fusion
  707.0 1.4 reshape.235
  708.3 2.1 gather_fusion.1
  710.4 2.6 select_convert_fusion
  713.0 3.3 reshape.242
  716.3 3.7 reduce_sum.137
  720.0 1.3 fusion.31
  721.3 2.3 fusion.34
  723.5 1.8 collective-permute-start.1
  725.3 180.8 %all-to-all-done.1 = bf16[32,36,3584]{2,1,0:T(8,128)(2,1)} async-done(((bf16[32,36,3584]{2,1,0:T(8,128)(2,1)}), bf16[32,36,3584]{2,1,0:T(8,128)(2,1)}, u32[]{:S(2)}, u32[]{:S(2)}) %all-to-all-start.1) | async-done | bytes 8257568 | tf_op jit(solution)/shard_map/all_to_all | solution.py:35
  906.1 6.3 bitcast_reduce_fusion.1
  912.4 1.4 reshape.229
  913.8 2.1 gather_fusion
  915.8 2.6 select_convert_fusion.1
  918.5 3.3 reshape.237
  921.7 4.1 multiply_reduce_fusion
  925.9 2.4 collective-permute-start
  928.3 5.4 collective-permute-done
  934.5 1.8 copy.65
  (51 shorter events, 4.3 us)
Async XLA Ops:
  0.6 287.6 %copy-start = (bf16[1,1,3584,256]{3,2,1,0:T(8,128)(2,1)S(1)}, bf16[1,1,3584,256]{3,2,1,0:T(8,128)(2,1)}, u32[]{:S(2)}) copy-start(bf16[1,1,3584,256]{3,2,1,0:T(8,128)(2,1)} %param.24) | copy-start | bytes 5505028
  17.7 12.3 %copy-start.6 = (s32[1,64,2]{1,2,0:T(2,128)S(1)}, s32[1,64,2]{1,2,0:T(2,128)}, u32[]{:S(2)}) copy-start(s32[1,64,2]{1,2,0:T(2,128)} %param.15) | copy-start | bytes 1540
  17.7 12.6 %copy-start.5 = (f32[1,3584]{1,0:T(1,128)S(1)}, f32[1,3584]{1,0:T(1,128)}, u32[]{:S(2)}) copy-start(f32[1,3584]{1,0:T(1,128)} %param.22) | copy-start | bytes 43012
  17.7 12.8 %copy-start.1 = (bf16[1,64,3584]{2,1,0:T(8,128)(2,1)S(1)}, bf16[1,64,3584]{2,1,0:T(8,128)(2,1)}, u32[]{:S(2)}) copy-start(bf16[1,64,3584]{2,1,0:T(8,128)(2,1)} %param.14) | copy-start | bytes 1376260
  17.7 219.8 %all-to-all-start.2 = ((bf16[32,36,3584]{2,1,0:T(8,128)(2,1)}), bf16[32,36,3584]{2,1,0:T(8,128)(2,1)}, u32[]{:S(2)}, u32[]{:S(2)}) async-start(bf16[32,36,3584]{2,1,0:T(8,128)(2,1)} %bitcast.79), calls=%async_computation.2 | async-start | bytes 18350080 | tf_op jit(solution)/shard_map/all_to_all | solution.py:89
  241.7 15.9 %copy-start.4 = (bf16[1,1,1152,2,256]{4,3,2,1,0:T(2,128)(2,1)S(1)}, bf16[1,1,1152,2,256]{4,3,2,1,0:T(2,128)(2,1)}, u32[]{:S(2)}) copy-start(bf16[1,1,1152,2,256]{4,3,2,1,0:T(2,128)(2,1)} %param.21) | copy-start | bytes 3538948
  241.7 221.8 %all-to-all-start = ((bf16[32,36,3584]{2,1,0:T(8,128)(2,1)}), bf16[32,36,3584]{2,1,0:T(8,128)(2,1)}, u32[]{:S(2)}, u32[]{:S(2)}) async-start(bf16[32,36,3584]{2,1,0:T(8,128)(2,1)} %bitcast.80), calls=%async_computation | async-start | bytes 18350080 | tf_op jit(solution)/shard_map/all_to_all | solution.py:88
  273.6 6.3 copy-start.2
  273.6 6.4 copy-start.3
  463.6 221.7 %all-to-all-start.3 = ((bf16[32,36,3584]{2,1,0:T(8,128)(2,1)}), bf16[32,36,3584]{2,1,0:T(8,128)(2,1)}, u32[]{:S(2)}, u32[]{:S(2)}) async-start(bf16[32,36,3584]{2,1,0:T(8,128)(2,1)} %reshape.233), calls=%async_computation.3 | async-start | bytes 18350080 | tf_op jit(solution)/shard_map/all_to_all | solution.py:35
  523.6 176.9 %copy-start.7 = (f32[1,64,2]{1,2,0:T(2,128)S(1)}, f32[1,64,2]{1,2,0:T(2,128)}, u32[]{:S(2)}) copy-start(f32[1,64,2]{1,2,0:T(2,128)} %param.16) | copy-start | bytes 1540
  685.3 220.9 %all-to-all-start.1 = ((bf16[32,36,3584]{2,1,0:T(8,128)(2,1)}), bf16[32,36,3584]{2,1,0:T(8,128)(2,1)}, u32[]{:S(2)}, u32[]{:S(2)}) async-start(bf16[32,36,3584]{2,1,0:T(8,128)(2,1)} %reshape.227), calls=%async_computation.1 | async-start | bytes 18350080 | tf_op jit(solution)/shard_map/all_to_all | solution.py:35
  723.5 204.7 %collective-permute-start.1 = (bf16[64,3584]{1,0:T(8,128)(2,1)}, bf16[64,3584]{1,0:T(8,128)(2,1)}, u32[]{:S(2)}, u32[]{:S(2)}) collective-permute-start(bf16[64,3584]{1,0:T(8,128)(2,1)} %fusion.34), channel_id=1, source_target_pairs={{0,224},{32,0},{64,32},{96,64},{128,96},{160,128},{192,160},{224,1... | collective-permute-start | bytes 1376264 | tf_op jit(solution)/shard_map/ppermute | solution.py:11
  925.9 7.8 collective-permute-start
where the time goes:
time: 946 us; the launch traced here: 936 us
  waiting for transfers between devices  703 us (74%)
  local copies, waits for them, and re-layouts  84 us (9%)
  starting transfers between devices  62.4 us (7%)
  matrix products  49.8 us (5%)
  other arithmetic  36 us (4%)
    all_to_all x2, waiting for transfers between devices, return_flat(): lax.all_to_all(block, ('node', 'local'), split_axis=0, concat_axis=0, til...  342 us
    all_to_all x1, waiting for transfers between devices, local(): lax.all_to_all(wide_second, ('node', 'local'), split_axis=0, concat_axis=...  204 us
    all_to_all x1, waiting for transfers between devices, local(): lax.all_to_all(wide_first, ('node', 'local'), split_axis=0, concat_axis=0...  151 us
    all_to_all x2, starting transfers between devices, return_flat(): lax.all_to_all(block, ('node', 'local'), split_axis=0, concat_axis=0, til...  30.1 us
  transfers between devices with their start and end apart: 6, of which 5 were waited for; matrix products, arithmetic and copies ran while one was open for 16% of the time, Pallas kernels for 0%

commit v1 on v0

v1 whole, which is shorter than its diff:
```python
import jax
import jax.numpy as jnp
from jax import lax
from jax.sharding import PartitionSpec as P

EPSILON = 1e-06
Y_SIZE = 4
PARTS = 4
META = 128
BF16 = jnp.bfloat16
F32 = jnp.float32
FEATURES_LAST = (((1,), (1,)), ((), ()))
ROWS_FIRST = (((0,), (0,)), ((), ()))
Z_ORDER = (0, -1, 1, -2, 2, -3, 3, 4)


def shift_y(value, by):
    count = lax.axis_size("local")
    pairs = [(i, i // Y_SIZE * Y_SIZE + (i % Y_SIZE + by) % Y_SIZE) for i in range(count)]
    return lax.ppermute(value, "local", pairs)


def shift_z(value, by):
    nodes = lax.axis_size("node")
    locals_ = lax.axis_size("local")
    depth = nodes * (locals_ // Y_SIZE)
    pairs = []
    for node in range(nodes):
        for place in range(locals_):
            z = (place // Y_SIZE) * nodes + node
            to = (z + by) % depth
            pairs.append(
                (node * locals_ + place, (to % nodes) * locals_ + to // nodes * Y_SIZE + place % Y_SIZE)
            )
    return lax.ppermute(value, ("node", "local"), pairs)


def shift_section(value, by):
    size = lax.axis_size("section")
    return lax.ppermute(value, "section", [(i, (i + by) % size) for i in range(size)])


def rms_scale(values):
    return lax.rsqrt(jnp.mean(values * values, axis=-1, keepdims=True) + EPSILON)


def gather_z(block, flip):
    got = {0: block}
    for step in range(1, 5 if not flip else 4):
        got[-step] = shift_z(got[-(step - 1)], 1)
    for step in range(1, 4 if not flip else 5):
        got[step] = shift_z(got[step - 1], -1)
    got[4] = got[4] if 4 in got else got[-4]
    return [got[i] for i in Z_ORDER]


def gather_y(block, flip):
    before = shift_y(block, 1)
    after = shift_y(block, -1)
    far = shift_y(after, -1) if flip else shift_y(before, 1)
    return {0: block, -1: before, 1: after, 2: far}


def scatter_y(term, flip):
    side = -1 if flip else 1
    far = shift_y(term(2).astype(BF16), side)
    through = shift_y((term(side) + far.astype(F32)).astype(BF16), side)
    direct = shift_y(term(-side).astype(BF16), -side)
    return term(0) + through.astype(F32) + direct.astype(F32)


def scatter_z(term, flip):
    side = -1 if flip else 1
    long = shift_z(term(4).astype(BF16), side)
    for step in (3, 2, 1):
        long = shift_z((term(side * step) + long.astype(F32)).astype(BF16), side)
    short = shift_z(term(-side * 3).astype(BF16), -side)
    for step in (2, 1):
        short = shift_z((term(-side * step) + short.astype(F32)).astype(BF16), -side)
    return term(0) + long.astype(F32) + short.astype(F32)


def slots_of(route, experts):
    named = route[:, :, None] == jnp.arange(experts, dtype=jnp.int32)[None, None, :]
    chosen = jnp.any(named, axis=1)
    rows = route.shape[0]
    earlier = lax.broadcasted_iota(jnp.int32, (rows, rows), 1) < lax.broadcasted_iota(
        jnp.int32, (rows, rows), 0
    )
    before = jnp.dot(earlier.astype(BF16), chosen.astype(BF16), preferred_element_type=F32)
    return named, jnp.where(chosen, before, -1.0)


def split_three(value):
    first = value.astype(BF16)
    rest = value - first.astype(F32)
    second = rest.astype(BF16)
    third = (rest - second.astype(F32)).astype(BF16)
    return [first, second, third]


def describe(route, weight, experts):
    named, slot = slots_of(route, experts)
    spread = jnp.sum(jnp.where(named, weight[:, :, None], 0.0), axis=1)
    return [slot.astype(BF16)] + split_three(spread)


def local(
    x_fwd,
    route_fwd,
    weight_fwd,
    x_bwd,
    grad_out,
    route_bwd,
    weight_bwd,
    saved_pre,
    norm_gain,
    w_gate,
    w_up,
    w_down,
):
    experts = lax.axis_size("node")
    halves = lax.axis_size("local") // Y_SIZE
    depth = experts * halves
    tokens, width = x_fwd.shape[1:]
    units = w_gate.shape[3]
    slot_total = saved_pre.shape[2]
    capacity = slot_total // (depth * Y_SIZE)
    group = depth * capacity
    part = width // PARTS
    expert = lax.axis_index("node")
    place = lax.axis_index("local")
    my_y = place % Y_SIZE
    my_z = place // Y_SIZE * experts + expert

    both_w = jnp.concatenate([w_gate[0, 0], w_up[0, 0]], axis=1)
    down_w = w_down[0, 0]
    gain = norm_gain[0]
    upstream = grad_out[0]

    def columns(value, c):
        return value[:, c * part : (c + 1) * part]

    pieces = describe(route_fwd[0], weight_fwd[0], experts) + describe(
        route_bwd[0], weight_bwd[0], experts
    )
    meta = jnp.concatenate(pieces, axis=1)
    meta = jnp.pad(meta, ((0, 0), (0, META - meta.shape[1])))

    gathered = [
        gather_z(
            jnp.concatenate([columns(upstream, 0), meta], axis=1) if c == 0 else columns(upstream, c),
            c % 2 == 1,
        )
        for c in range(PARTS)
    ]
    x_first = x_fwd[0].astype(F32)
    normed = (x_first * rms_scale(x_first) * gain).astype(BF16)
    gathered_first = [gather_z(columns(normed, c), c % 2 == 1) for c in range(PARTS)]

    stacked = [jnp.concatenate(blocks, axis=0) for blocks in gathered]
    metas = stacked[0][:, part:]
    mine = lax.broadcasted_iota(jnp.int32, (1, experts), 1) == expert

    def pick(values, index):
        cut = values[:, index * experts : (index + 1) * experts].astype(F32)
        return jnp.sum(jnp.where(mine, cut, 0.0), axis=1, keepdims=True)

    z_of = jnp.concatenate(
        [jnp.full((tokens, 1), (my_z + i + depth) % depth, jnp.int32) for i in Z_ORDER], axis=0
    )

    def table(index):
        slot = pick(metas, index).astype(jnp.int32)
        target = jnp.where(slot >= 0, z_of * capacity + slot, -1)
        return (
            target == lax.broadcasted_iota(jnp.int32, (depth * tokens, group), 1)
        ).astype(BF16)

    table_first = table(0)
    table_second = table(4)

    def choose(chosen, values):
        return lax.dot_general(chosen, values, ROWS_FIRST, preferred_element_type=F32)

    def weights_of(picked, index):
        return pick(picked, index + 1) + pick(picked, index + 2) + pick(picked, index + 3)

    opening = choose(table_second, stacked[0])
    slot_weight_second = weights_of(opening[:, part:], 4)
    slot_weight_first = weights_of(choose(table_first, metas), 0)

    arrived_second = []
    for c in range(PARTS):
        rows = opening[:, :part] if c == 0 else choose(table_second, stacked[c])
        arrived_second.append(gather_y((rows * slot_weight_second).astype(BF16), c % 2 == 1))
    arrived_first = []
    for c in range(PARTS):
        rows = choose(table_first, jnp.concatenate(gathered_first[c], axis=0))
        arrived_first.append(gather_y(rows.astype(BF16), c % 2 == 1))

    saved = saved_pre[0, 0].reshape(halves, Y_SIZE, experts * capacity, 2, units)
    pre_grads = {}
    for r in (2, 1, -1, 0):
        hidden_grad = sum(
            lax.dot_general(
                arrived_second[c][r], columns(down_w, c), FEATURES_LAST, preferred_element_type=F32
            )
            for c in range(PARTS)
        )
        stored = lax.dynamic_index_in_dim(
            saved, (my_y + r + Y_SIZE) % Y_SIZE, 1, keepdims=False
        ).reshape(group, 2, units)
        gate = stored[:, 0, :].astype(F32)
        upper = stored[:, 1, :].astype(F32)
        sigma = jax.nn.sigmoid(gate)
        grad_gate = hidden_grad * upper * sigma * (1.0 + gate * (1.0 - sigma))
        grad_upper = hidden_grad * gate * sigma
        pre_grads[r] = jnp.concatenate([grad_gate, grad_upper], axis=1).astype(BF16)

    hidden = {}
    for r in (2, 1, -1, 0):
        both = sum(
            jnp.dot(
                arrived_first[c][r],
                both_w[c * part : (c + 1) * part],
                preferred_element_type=F32,
            )
            for c in range(PARTS)
        )
        hidden[r] = (jax.nn.silu(both[:, :units]) * both[:, units:]).astype(BF16)

    def give_back(chosen, rows, flip):
        rows = rows.astype(BF16)

        def term(i):
            at = Z_ORDER.index(i) * tokens
            return jnp.dot(chosen[at : at + tokens], rows, preferred_element_type=F32)

        return scatter_z(term, flip)

    normed_grad = []
    for c in range(PARTS):
        rows = scatter_y(
            lambda r: lax.dot_general(
                pre_grads[r],
                both_w[c * part : (c + 1) * part],
                FEATURES_LAST,
                preferred_element_type=F32,
            ),
            c % 2 == 1,
        )
        normed_grad.append(give_back(table_second, rows, c % 2 == 1))

    x_second = x_bwd[0].astype(F32)
    scale = rms_scale(x_second)
    along = gain * jnp.concatenate(normed_grad, axis=1)
    input_grad = (
        upstream.astype(F32)
        + scale * along
        - x_second * (scale * scale * scale) * jnp.mean(along * x_second, axis=-1, keepdims=True)
    )
    grad_prev = shift_section(input_grad.astype(BF16), -1)

    act_next = []
    for c in range(PARTS):
        rows = scatter_y(
            lambda r: jnp.dot(hidden[r], columns(down_w, c), preferred_element_type=F32),
            c % 2 == 1,
        )
        added = give_back(table_first, rows * slot_weight_first, c % 2 == 1)
        act_next.append(shift_section((columns(x_first, c) + added).astype(BF16), 1))
    return (jnp.concatenate(act_next, axis=1)[None], grad_prev[None])


def solution(mesh):
    tokens = P("section", ("node", "local"), None)
    in_specs = (
        tokens,
        tokens,
        tokens,
        tokens,
        tokens,
        tokens,
        tokens,
        P("section", "node", None, None, "local"),
        P("section", None),
        P("section", "node", None, "local"),
        P("section", "node", None, "local"),
        P("section", "node", "local", None),
    )
    return jax.shard_map(
        local, mesh=mesh, in_specs=in_specs, out_specs=(tokens, tokens), check_vma=False
    )
```

time: 946 us -> 580 us (0.61)
  waiting for transfers between devices: 703 us -> 210 us
  starting transfers between devices: 62.4 us -> 259 us
  local copies, waits for them, and re-layouts: 84 us -> 35.2 us
  other arithmetic: 36 us -> 14.3 us
    all_to_all x4 -> x0, waiting for transfers between devices: 698 us -> none  [the longest x2 342 us: return_flat(): lax.all_to_all(block, ('node', 'local'), split_axis=0, concat_axis=0, til...]
    ppermute x2 -> x165, starting transfers between devices: 4.15 us -> 259 us  [the longest x112 131 us: shift_z(): return lax.ppermute(value, ('node', 'local'), pairs)]
    ppermute x2 -> x165, waiting for transfers between devices: 5.42 us -> 210 us  [the longest x48 165 us: shift_y(): return lax.ppermute(value, 'local', pairs)]
    all_to_all x4 -> x0, starting transfers between devices: 58.2 us -> none  [the longest x2 30.1 us: return_flat(): lax.all_to_all(block, ('node', 'local'), split_axis=0, concat_axis=0, til...]
    reshape x6 -> x0, local copies, waits for them, and re-layouts: 53 us -> none  [the longest x1 12.6 us: local(): arrived_second = got_second.reshape(slot_total, feature_width)]
    unnamed x18 -> x86, local copies, waits for them, and re-layouts: 2.62 us -> 27.1 us
    reduce_sum x9 -> x4, other arithmetic: 21.9 us -> 3.28 us  [the longest x2 1.87 us: pick(): return jnp.sum(jnp.where(mine, cut, 0.0), axis=1, keepdims=True)]
    broadcast_in_dim x4 -> x8, local copies, waits for them, and re-layouts: 11 us -> 0.02 us  [local(): jnp.full((tokens, 1), (my_z + i + depth) % depth, jnp.int32)]
  transfers between devices with their start and end apart: 6 -> 165, of which waited for: 5 -> 46; matrix products, arithmetic and copies ran while one was open for 16% -> 15% of each run, Pallas kernels for 0% -> 0%
where the time goes in v1:
time: 580 us; the launch traced here: 571 us
  starting transfers between devices  259 us (45%)
  waiting for transfers between devices  210 us (36%)
  matrix products  49.2 us (8%)
  local copies, waits for them, and re-layouts  35.2 us (6%)
  other arithmetic  14.3 us (2%)
    ppermute x48, waiting for transfers between devices, shift_y(): return lax.ppermute(value, 'local', pairs)  165 us
    ppermute x112, starting transfers between devices, shift_z(): return lax.ppermute(value, ('node', 'local'), pairs)  131 us
    ppermute x5, starting transfers between devices, shift_section(): lax.ppermute(value, 'section', [(i, (i + by) % size) for i in range(size)])  76.5 us
    ppermute x48, starting transfers between devices, shift_y(): return lax.ppermute(value, 'local', pairs)  50.8 us
    ppermute x112, waiting for transfers between devices, shift_z(): return lax.ppermute(value, ('node', 'local'), pairs)  43.7 us
    unnamed x86, local copies, waits for them, and re-layouts  27.1 us
    dot_general x64, matrix products, term(): return jnp.dot(chosen[at:at + tokens], rows, preferred_element_type=F32)  14.9 us
  transfers between devices with their start and end apart: 165, of which 46 were waited for; matrix products, arithmetic and copies ran while one was open for 15% of the time, Pallas kernels for 0%

profile of v1, /device:TPU:1, one launch (start us, length us, event | category | flops | bytes accessed | tf_op | source)
XLA Modules:
  0.0 570.9 jit_solution(1808324000344441189)
XLA Ops:
  5.2 3.9 collective-permute-start.106
  17.5 3.1 fusion.80
  20.6 3.0 constant_dynamic-slice_fusion
  29.8 2.7 collective-permute-start.99
  89.7 2.8 collective-permute-start.114
  93.2 2.7 collective-permute-start.115
  101.0 4.8 collective-permute-done.115
  108.7 8.2 %collective-permute-done.113 = bf16[288,896]{1,0:T(8,128)(2,1)S(1)} collective-permute-done((bf16[288,896]{1,0:T(8,128)(2,1)S(1)}, bf16[288,896]{1,0:T(8,128)(2,1)S(1)}, u32[]{:S(2)}, u32[]{:S(2)}) %collective-permute-start.113) | collective-permute-done | bytes 516128 | tf_op jit(solution)/shard_map/ppermute | solution.py:20
  121.2 6.7 %collective-permute-done.112 = bf16[288,896]{1,0:T(8,128)(2,1)S(1)} collective-permute-done((bf16[288,896]{1,0:T(8,128)(2,1)S(1)}, bf16[288,896]{1,0:T(8,128)(2,1)S(1)}, u32[]{:S(2)}, u32[]{:S(2)}) %collective-permute-start.112) | collective-permute-done | bytes 516128 | tf_op jit(solution)/shard_map/ppermute | solution.py:20
  140.1 3.6 collective-permute-done.120
  144.1 6.0 %collective-permute-done.118 = bf16[288,896]{1,0:T(8,128)(2,1)S(1)} collective-permute-done((bf16[288,896]{1,0:T(8,128)(2,1)S(1)}, bf16[288,896]{1,0:T(8,128)(2,1)S(1)}, u32[]{:S(2)}, u32[]{:S(2)}) %collective-permute-start.118) | collective-permute-done | bytes 516128 | tf_op jit(solution)/shard_map/ppermute | solution.py:20
  150.4 15.4 %collective-permute-done.117 = bf16[288,896]{1,0:T(8,128)(2,1)S(1)} collective-permute-done((bf16[288,896]{1,0:T(8,128)(2,1)S(1)}, bf16[288,896]{1,0:T(8,128)(2,1)S(1)}, u32[]{:S(2)}, u32[]{:S(2)}) %collective-permute-start.117) | collective-permute-done | bytes 516128 | tf_op jit(solution)/shard_map/ppermute | solution.py:20
  169.8 8.0 %collective-permute-done.154 = bf16[288,896]{1,0:T(8,128)(2,1)S(1)} collective-permute-done((bf16[288,896]{1,0:T(8,128)(2,1)S(1)}, bf16[288,896]{1,0:T(8,128)(2,1)S(1)}, u32[]{:S(2)}, u32[]{:S(2)}) %collective-permute-start.154) | collective-permute-done | bytes 516128 | tf_op jit(solution)/shard_map/ppermute | solution.py:20
  177.8 3.5 collective-permute-start.134
  181.8 6.1 %collective-permute-done.144 = bf16[288,896]{1,0:T(8,128)(2,1)S(1)} collective-permute-done((bf16[288,896]{1,0:T(8,128)(2,1)S(1)}, bf16[288,896]{1,0:T(8,128)(2,1)S(1)}, u32[]{:S(2)}, u32[]{:S(2)}) %collective-permute-start.144) | collective-permute-done | bytes 516128 | tf_op jit(solution)/shard_map/ppermute | solution.py:20
  188.5 2.8 collective-permute-start.155
  191.7 11.3 %collective-permute-done.122 = bf16[288,896]{1,0:T(8,128)(2,1)S(1)} collective-permute-done((bf16[288,896]{1,0:T(8,128)(2,1)S(1)}, bf16[288,896]{1,0:T(8,128)(2,1)S(1)}, u32[]{:S(2)}, u32[]{:S(2)}) %collective-permute-start.122) | collective-permute-done | bytes 516128 | tf_op jit(solution)/shard_map/ppermute | solution.py:20
  207.3 6.3 %collective-permute-done.145 = bf16[288,896]{1,0:T(8,128)(2,1)S(1)} collective-permute-done((bf16[288,896]{1,0:T(8,128)(2,1)S(1)}, bf16[288,896]{1,0:T(8,128)(2,1)S(1)}, u32[]{:S(2)}, u32[]{:S(2)}) %collective-permute-start.145) | collective-permute-done | bytes 516128 | tf_op jit(solution)/shard_map/ppermute | solution.py:20
  214.2 8.0 %collective-permute-done.135 = bf16[288,896]{1,0:T(8,128)(2,1)S(1)} collective-permute-done((bf16[288,896]{1,0:T(8,128)(2,1)S(1)}, bf16[288,896]{1,0:T(8,128)(2,1)S(1)}, u32[]{:S(2)}, u32[]{:S(2)}) %collective-permute-start.135) | collective-permute-done | bytes 516128 | tf_op jit(solution)/shard_map/ppermute | solution.py:20
  228.1 2.9 collective-permute-start.137
  250.4 3.1 collective-permute-start.139
  258.0 4.6 collective-permute-done.129
  272.1 3.1 collective-permute-done.130
  279.2 2.9 collective-permute-start.22
  302.2 3.1 collective-permute-start.26
  315.6 3.7 collective-permute-done.13
  328.7 6.2 %collective-permute-done.48 = bf16[288,896]{1,0:T(8,128)(2,1)S(1)} collective-permute-done((bf16[288,896]{1,0:T(8,128)(2,1)S(1)}, bf16[288,896]{1,0:T(8,128)(2,1)S(1)}, u32[]{:S(2)}, u32[]{:S(2)}) %collective-permute-start.48) | collective-permute-done | bytes 516128 | tf_op jit(solution)/shard_map/ppermute | solution.py:20
  335.4 4.9 collective-permute-done.42
  340.7 5.1 collective-permute-done.47
  349.6 4.3 collective-permute-done.35
  359.9 8.8 %collective-permute-done.44 = bf16[288,896]{1,0:T(8,128)(2,1)S(1)} collective-permute-done((bf16[288,896]{1,0:T(8,128)(2,1)S(1)}, bf16[288,896]{1,0:T(8,128)(2,1)S(1)}, u32[]{:S(2)}, u32[]{:S(2)}) %collective-permute-start.44) | collective-permute-done | bytes 516128 | tf_op jit(solution)/shard_map/ppermute | solution.py:20
  369.2 12.1 %collective-permute-done.43 = bf16[288,896]{1,0:T(8,128)(2,1)S(1)} collective-permute-done((bf16[288,896]{1,0:T(8,128)(2,1)S(1)}, bf16[288,896]{1,0:T(8,128)(2,1)S(1)}, u32[]{:S(2)}, u32[]{:S(2)}) %collective-permute-start.43) | collective-permute-done | bytes 516128 | tf_op jit(solution)/shard_map/ppermute | solution.py:20
  382.6 14.1 %collective-permute-done.40 = bf16[288,896]{1,0:T(8,128)(2,1)S(1)} collective-permute-done((bf16[288,896]{1,0:T(8,128)(2,1)S(1)}, bf16[288,896]{1,0:T(8,128)(2,1)S(1)}, u32[]{:S(2)}, u32[]{:S(2)}) %collective-permute-start.40) | collective-permute-done | bytes 516128 | tf_op jit(solution)/shard_map/ppermute | solution.py:20
  401.4 5.4 collective-permute-done.45
  407.1 5.2 collective-permute-done.58
  412.3 3.4 collective-permute-start.80
  416.5 10.9 %collective-permute-done.80 = bf16[288,896]{1,0:T(8,128)(2,1)S(1)} collective-permute-done((bf16[288,896]{1,0:T(8,128)(2,1)S(1)}, bf16[288,896]{1,0:T(8,128)(2,1)S(1)}, u32[]{:S(2)}, u32[]{:S(2)}) %collective-permute-start.80) | collective-permute-done | bytes 516128 | tf_op jit(solution)/shard_map/ppermute | solution.py:20
  427.7 3.5 collective-permute-start.59
  434.5 50.7 %collective-permute-start.164 = (bf16[64,3584]{1,0:T(8,128)(2,1)S(1)}, bf16[64,3584]{1,0:T(8,128)(2,1)S(1)}, u32[]{:S(2)}, u32[]{:S(2)}) collective-permute-start(bf16[64,3584]{1,0:T(8,128)(2,1)S(1)} %get-tuple-element.48), channel_id=1, source_target_pairs={{0,224},{32,0},{64,32},{96,64},{128,96},{160,128},{192,160},{224,1... | collective-permute-start | bytes 1376264 | tf_op jit(solution)/shard_map/ppermute | solution.py:40
  493.3 3.0 collective-permute-start.61
  511.5 2.7 collective-permute-start.85
  517.6 3.1 collective-permute-done.74
  521.0 4.5 collective-permute-done.63
  525.7 6.1 %collective-permute-done.52 = bf16[64,896]{1,0:T(8,128)(2,1)S(1)} collective-permute-done((bf16[64,896]{1,0:T(8,128)(2,1)S(1)}, bf16[64,896]{1,0:T(8,128)(2,1)S(1)}, u32[]{:S(2)}, u32[]{:S(2)}) %collective-permute-start.52) | collective-permute-done | bytes 114720 | tf_op jit(solution)/shard_map/ppermute | solution.py:35
  532.1 3.6 collective-permute-done.86
  536.0 2.7 collective-permute-start.64
  540.8 20.3 %collective-permute-start.90 = (bf16[64,896]{1,0:T(8,128)(2,1)S(1)}, bf16[64,896]{1,0:T(8,128)(2,1)S(1)}, u32[]{:S(2)}, u32[]{:S(2)}) collective-permute-start(bf16[64,896]{1,0:T(8,128)(2,1)S(1)} %fusion.27), channel_id=1, source_target_pairs={{0,32},{32,64},{64,96},{96,128},{128,160},{160,192},{192,224},{224... | collective-permute-start | bytes 344072 | tf_op jit(solution)/shard_map/ppermute | solution.py:40
  563.2 3.9 collective-permute-start.57
  (562 shorter events, 250.7 us)
Async XLA Ops:
  2.7 27.1 %collective-permute-start.105 = (bf16[64,896]{1,0:T(8,128)(2,1)}, bf16[64,896]{1,0:T(8,128)(2,1)}, u32[]{:S(2)}, u32[]{:S(2)}) collective-permute-start(bf16[64,896]{1,0:T(8,128)(2,1)} %get-tuple-element.36), channel_id=1, source_target_pairs={{0,8},{1,9},{2,10},{3,11},{4,12},{5,13},{6,14},{7,15},{8,16},{9,17... | collective-permute-start | bytes 344072 | tf_op jit(solution)/shard_map/ppermute | solution.py:35
  5.2 28.9 %collective-permute-start.106 = (bf16[64,896]{1,0:T(8,128)(2,1)}, bf16[64,896]{1,0:T(8,128)(2,1)}, u32[]{:S(2)}, u32[]{:S(2)}) collective-permute-start(bf16[64,896]{1,0:T(8,128)(2,1)} %get-tuple-element.36), channel_id=1, source_target_pairs={{0,28},{1,29},{2,30},{3,31},{4,24},{5,25},{6,26},{7,27},{8,0},{9,1... | collective-permute-start | bytes 344072 | tf_op jit(solution)/shard_map/ppermute | solution.py:35
  13.1 31.4 %collective-permute-start = (bf16[64,1024]{1,0:T(8,128)(2,1)S(1)}, bf16[64,1024]{1,0:T(8,128)(2,1)}, u32[]{:S(2)}, u32[]{:S(2)}) collective-permute-start(bf16[64,1024]{1,0:T(8,128)(2,1)S(1)} %get-tuple-element.46), channel_id=1, source_target_pairs={{0,8},{1,9},{2,10},{3,11},{4,12},{5,13},{6,14},{7,15},{8,16},{9,17... | collective-permute-start | bytes 393224 | tf_op jit(solution)/shard_map/ppermute | solution.py:35
  13.1 35.6 %collective-permute-start.1 = (bf16[64,1024]{1,0:T(8,128)(2,1)S(1)}, bf16[64,1024]{1,0:T(8,128)(2,1)S(1)}, u32[]{:S(2)}, u32[]{:S(2)}) collective-permute-start(bf16[64,1024]{1,0:T(8,128)(2,1)S(1)} %get-tuple-element.46), channel_id=1, source_target_pairs={{0,28},{1,29},{2,30},{3,31},{4,24},{5,25},{6,26},{7,27},{8,0},{9,1... | collective-permute-start | bytes 393224 | tf_op jit(solution)/shard_map/ppermute | solution.py:35
  15.8 19.8 %collective-permute-start.98 = (bf16[64,896]{1,0:T(8,128)(2,1)}, bf16[64,896]{1,0:T(8,128)(2,1)}, u32[]{:S(2)}, u32[]{:S(2)}) collective-permute-start(bf16[64,896]{1,0:T(8,128)(2,1)} %get-tuple-element.35), channel_id=1, source_target_pairs={{0,8},{1,9},{2,10},{3,11},{4,12},{5,13},{6,14},{7,15},{8,16},{9,17... | collective-permute-start | bytes 344072 | tf_op jit(solution)/shard_map/ppermute | solution.py:35
  89.7 17.2 %collective-permute-start.114 = (bf16[288,896]{1,0:T(8,128)(2,1)S(1)}, bf16[288,896]{1,0:T(8,128)(2,1)S(1)}, u32[]{:S(2)}, u32[]{:S(2)}) collective-permute-start(bf16[288,896]{1,0:T(8,128)(2,1)S(1)} %fusion.1), channel_id=1, source_target_pairs={{0,3},{1,0},{2,1},{3,2},{4,7},{5,4},{6,5},{7,6},{8,11},{9,8},{10,9... | collective-permute-start | bytes 1548296 | tf_op jit(solution)/shard_map/ppermute | solution.py:20
  92.5 25.6 %collective-permute-start.119 = (bf16[288,896]{1,0:T(8,128)(2,1)S(1)}, bf16[288,896]{1,0:T(8,128)(2,1)S(1)}, u32[]{:S(2)}, u32[]{:S(2)}) collective-permute-start(bf16[288,896]{1,0:T(8,128)(2,1)S(1)} %fusion.1), channel_id=1, source_target_pairs={{0,1},{1,2},{2,3},{3,0},{4,5},{5,6},{6,7},{7,4},{8,9},{9,10},{10,1... | collective-permute-start | bytes 1548296 | tf_op jit(solution)/shard_map/ppermute | solution.py:20
  96.6 20.3 %collective-permute-start.113 = (bf16[288,896]{1,0:T(8,128)(2,1)S(1)}, bf16[288,896]{1,0:T(8,128)(2,1)S(1)}, u32[]{:S(2)}, u32[]{:S(2)}) collective-permute-start(bf16[288,896]{1,0:T(8,128)(2,1)S(1)} %fusion), channel_id=1, source_target_pairs={{0,3},{1,0},{2,1},{3,2},{4,7},{5,4},{6,5},{7,6},{8,11},{9,8},{10,9... | collective-permute-start | bytes 1548296 | tf_op jit(solution)/shard_map/ppermute | solution.py:20
  96.7 31.2 %collective-permute-start.112 = (bf16[288,896]{1,0:T(8,128)(2,1)S(1)}, bf16[288,896]{1,0:T(8,128)(2,1)S(1)}, u32[]{:S(2)}, u32[]{:S(2)}) collective-permute-start(bf16[288,896]{1,0:T(8,128)(2,1)S(1)} %fusion.73), channel_id=1, source_target_pairs={{0,3},{1,0},{2,1},{3,2},{4,7},{5,4},{6,5},{7,6},{8,11},{9,8},{10,9... | collective-permute-start | bytes 1548296 | tf_op jit(solution)/shard_map/ppermute | solution.py:20
  105.8 27.8 %collective-permute-start.116 = (bf16[288,896]{1,0:T(8,128)(2,1)S(1)}, bf16[288,896]{1,0:T(8,128)(2,1)S(1)}, u32[]{:S(2)}, u32[]{:S(2)}) collective-permute-start(bf16[288,896]{1,0:T(8,128)(2,1)S(1)} %fusion.73), channel_id=1, source_target_pairs={{0,1},{1,2},{2,3},{3,0},{4,5},{5,6},{6,7},{7,4},{8,9},{9,10},{10,1... | collective-permute-start | bytes 1548296 | tf_op jit(solution)/shard_map/ppermute | solution.py:20
  106.9 22.2 %collective-permute-start.125 = (bf16[288,896]{1,0:T(8,128)(2,1)S(1)}, bf16[288,896]{1,0:T(8,128)(2,1)S(1)}, u32[]{:S(2)}, u32[]{:S(2)}) collective-permute-start(bf16[288,896]{1,0:T(8,128)(2,1)S(1)} %fusion.2), channel_id=1, source_target_pairs={{0,1},{1,2},{2,3},{3,0},{4,5},{5,6},{6,7},{7,4},{8,9},{9,10},{10,1... | collective-permute-start | bytes 1548296 | tf_op jit(solution)/shard_map/ppermute | solution.py:20
  116.9 15.9 %collective-permute-start.124 = (bf16[288,896]{1,0:T(8,128)(2,1)S(1)}, bf16[288,896]{1,0:T(8,128)(2,1)S(1)}, u32[]{:S(2)}, u32[]{:S(2)}) collective-permute-start(bf16[288,896]{1,0:T(8,128)(2,1)S(1)} %fusion), channel_id=1, source_target_pairs={{0,1},{1,2},{2,3},{3,0},{4,5},{5,6},{6,7},{7,4},{8,9},{9,10},{10,1... | collective-permute-start | bytes 1548296 | tf_op jit(solution)/shard_map/ppermute | solution.py:20
  118.1 20.8 %collective-permute-start.121 = (bf16[288,896]{1,0:T(8,128)(2,1)S(1)}, bf16[288,896]{1,0:T(8,128)(2,1)S(1)}, u32[]{:S(2)}, u32[]{:S(2)}) collective-permute-start(bf16[288,896]{1,0:T(8,128)(2,1)S(1)} %collective-permute-done.115), channel_id=1, source_target_pairs={{0,3},{1,0},{2,1},{3,2},{4,7},{5,4},{6,5},{7,6},{8,11},{9,8},{10,9... | collective-permute-start | bytes 1548296 | tf_op jit(solution)/shard_map/ppermute | solution.py:20
  127.9 15.8 %collective-permute-start.120 = (bf16[288,896]{1,0:T(8,128)(2,1)S(1)}, bf16[288,896]{1,0:T(8,128)(2,1)S(1)}, u32[]{:S(2)}, u32[]{:S(2)}) collective-permute-start(bf16[288,896]{1,0:T(8,128)(2,1)S(1)} %collective-permute-done.119), channel_id=1, source_target_pairs={{0,1},{1,2},{2,3},{3,0},{4,5},{5,6},{6,7},{7,4},{8,9},{9,10},{10,1... | collective-permute-start | bytes 1548296 | tf_op jit(solution)/shard_map/ppermute | solution.py:20
  129.1 20.9 %collective-permute-start.118 = (bf16[288,896]{1,0:T(8,128)(2,1)S(1)}, bf16[288,896]{1,0:T(8,128)(2,1)S(1)}, u32[]{:S(2)}, u32[]{:S(2)}) collective-permute-start(bf16[288,896]{1,0:T(8,128)(2,1)S(1)} %collective-permute-done.113), channel_id=1, source_target_pairs={{0,3},{1,0},{2,1},{3,2},{4,7},{5,4},{6,5},{7,6},{8,11},{9,8},{10,9... | collective-permute-start | bytes 1548296 | tf_op jit(solution)/shard_map/ppermute | solution.py:20
  135.1 68.6 %collective-permute-start.156 = (bf16[288,896]{1,0:T(8,128)(2,1)S(1)}, bf16[288,896]{1,0:T(8,128)(2,1)S(1)}, u32[]{:S(2)}, u32[]{:S(2)}) collective-permute-start(bf16[288,896]{1,0:T(8,128)(2,1)S(1)} %convolution_convert_fusion), channel_id=1, source_target_pairs={{0,1},{1,2},{2,3},{3,0},{4,5},{5,6},{6,7},{7,4},{8,9},{9,10},{10,1... | collective-permute-start | bytes 1548296 | tf_op jit(solution)/shard_map/ppermute | solution.py:20
  135.2 71.9 %collective-permute-start.146 = (bf16[288,896]{1,0:T(8,128)(2,1)S(1)}, bf16[288,896]{1,0:T(8,128)(2,1)S(1)}, u32[]{:S(2)}, u32[]{:S(2)}) collective-permute-start(bf16[288,896]{1,0:T(8,128)(2,1)S(1)} %convolution_convert_fusion.2), channel_id=1, source_target_pairs={{0,3},{1,0},{2,1},{3,2},{4,7},{5,4},{6,5},{7,6},{8,11},{9,8},{10,9... | collective-permute-start | bytes 1548296 | tf_op jit(solution)/shard_map/ppermute | solution.py:20
  139.0 26.8 %collective-permute-start.117 = (bf16[288,896]{1,0:T(8,128)(2,1)S(1)}, bf16[288,896]{1,0:T(8,128)(2,1)S(1)}, u32[]{:S(2)}, u32[]{:S(2)}) collective-permute-start(bf16[288,896]{1,0:T(8,128)(2,1)S(1)} %collective-permute-done.116), channel_id=1, source_target_pairs={{0,1},{1,2},{2,3},{3,0},{4,5},{5,6},{6,7},{7,4},{8,9},{9,10},{10,1... | collective-permute-start | bytes 1548296 | tf_op jit(solution)/shard_map/ppermute | solution.py:20
  143.7 70.5 %collective-permute-start.136 = (bf16[288,896]{1,0:T(8,128)(2,1)S(1)}, bf16[288,896]{1,0:T(8,128)(2,1)S(1)}, u32[]{:S(2)}, u32[]{:S(2)}) collective-permute-start(bf16[288,896]{1,0:T(8,128)(2,1)S(1)} %convolution_convert_fusion.4), channel_id=1, source_target_pairs={{0,1},{1,2},{2,3},{3,0},{4,5},{5,6},{6,7},{7,4},{8,9},{9,10},{10,1... | collective-permute-start | bytes 1548296 | tf_op jit(solution)/shard_map/ppermute | solution.py:20
  168.8 19.1 %collective-permute-start.144 = (bf16[288,896]{1,0:T(8,128)(2,1)S(1)}, bf16[288,896]{1,0:T(8,128)(2,1)S(1)}, u32[]{:S(2)}, u32[]{:S(2)}) collective-permute-start(bf16[288,896]{1,0:T(8,128)(2,1)S(1)} %convolution_convert_fusion.3), channel_id=1, source_target_pairs={{0,1},{1,2},{2,3},{3,0},{4,5},{5,6},{6,7},{7,4},{8,9},{9,10},{10,1... | collective-permute-start | bytes 1548296 | tf_op jit(solution)/shard_map/ppermute | solution.py:20
  188.5 16.6 %collective-permute-start.155 = (bf16[288,896]{1,0:T(8,128)(2,1)S(1)}, bf16[288,896]{1,0:T(8,128)(2,1)S(1)}, u32[]{:S(2)}, u32[]{:S(2)}) collective-permute-start(bf16[288,896]{1,0:T(8,128)(2,1)S(1)} %add_convert_fusion.1), channel_id=1, source_target_pairs={{0,3},{1,0},{2,1},{3,2},{4,7},{5,4},{6,5},{7,6},{8,11},{9,8},{10,9... | collective-permute-start | bytes 1548296 | tf_op jit(solution)/shard_map/ppermute | solution.py:20
  203.0 19.9 %collective-permute-start.126 = (bf16[288,896]{1,0:T(8,128)(2,1)S(1)}, bf16[288,896]{1,0:T(8,128)(2,1)S(1)}, u32[]{:S(2)}, u32[]{:S(2)}) collective-permute-start(bf16[288,896]{1,0:T(8,128)(2,1)S(1)} %convolution_convert_fusion.6), channel_id=1, source_target_pairs={{0,3},{1,0},{2,1},{3,2},{4,7},{5,4},{6,5},{7,6},{8,11},{9,8},{10,9... | collective-permute-start | bytes 1548296 | tf_op jit(solution)/shard_map/ppermute | solution.py:20
  205.1 17.2 %collective-permute-start.135 = (bf16[288,896]{1,0:T(8,128)(2,1)S(1)}, bf16[288,896]{1,0:T(8,128)(2,1)S(1)}, u32[]{:S(2)}, u32[]{:S(2)}) collective-permute-start(bf16[288,896]{1,0:T(8,128)(2,1)S(1)} %add_convert_fusion.5), channel_id=1, source_target_pairs={{0,3},{1,0},{2,1},{3,2},{4,7},{5,4},{6,5},{7,6},{8,11},{9,8},{10,9... | collective-permute-start | bytes 1548296 | tf_op jit(solution)/shard_map/ppermute | solution.py:20
  207.2 16.9 %collective-permute-start.123 = (bf16[288,896]{1,0:T(8,128)(2,1)S(1)}, bf16[288,896]{1,0:T(8,128)(2,1)S(1)}, u32[]{:S(2)}, u32[]{:S(2)}) collective-permute-start(bf16[288,896]{1,0:T(8,128)(2,1)S(1)} %add_convert_fusion.7), channel_id=1, source_target_pairs={{0,1},{1,2},{2,3},{3,0},{4,5},{5,6},{6,7},{7,4},{8,9},{9,10},{10,1... | collective-permute-start | bytes 1548296 | tf_op jit(solution)/shard_map/ppermute | solution.py:20
  244.2 19.8 %collective-permute-start.163 = (bf16[64,896]{1,0:T(8,128)(2,1)S(1)}, bf16[64,896]{1,0:T(8,128)(2,1)S(1)}, u32[]{:S(2)}, u32[]{:S(2)}) collective-permute-start(bf16[64,896]{1,0:T(8,128)(2,1)S(1)} %fusion.69), channel_id=1, source_target_pairs={{0,8},{1,9},{2,10},{3,11},{4,12},{5,13},{6,14},{7,15},{8,16},{9,17... | collective-permute-start | bytes 344072 | tf_op jit(solution)/shard_map/ppermute | solution.py:35
  247.6 21.3 %collective-permute-start.153 = (bf16[64,896]{1,0:T(8,128)(2,1)S(1)}, bf16[64,896]{1,0:T(8,128)(2,1)S(1)}, u32[]{:S(2)}, u32[]{:S(2)}) collective-permute-start(bf16[64,896]{1,0:T(8,128)(2,1)S(1)} %fusion.64), channel_id=1, source_target_pairs={{0,28},{1,29},{2,30},{3,31},{4,24},{5,25},{6,26},{7,27},{8,0},{9,1... | collective-permute-start | bytes 344072 | tf_op jit(solution)/shard_map/ppermute | solution.py:35
  250.1 19.4 %collective-permute-start.143 = (bf16[64,896]{1,0:T(8,128)(2,1)S(1)}, bf16[64,896]{1,0:T(8,128)(2,1)S(1)}, u32[]{:S(2)}, u32[]{:S(2)}) collective-permute-start(bf16[64,896]{1,0:T(8,128)(2,1)S(1)} %fusion.59), channel_id=1, source_target_pairs={{0,8},{1,9},{2,10},{3,11},{4,12},{5,13},{6,14},{7,15},{8,16},{9,17... | collective-permute-start | bytes 344072 | tf_op jit(solution)/shard_map/ppermute | solution.py:35
  254.8 17.4 %collective-permute-start.133 = (bf16[64,896]{1,0:T(8,128)(2,1)S(1)}, bf16[64,896]{1,0:T(8,128)(2,1)S(1)}, u32[]{:S(2)}, u32[]{:S(2)}) collective-permute-start(bf16[64,896]{1,0:T(8,128)(2,1)S(1)} %fusion.54), channel_id=1, source_target_pairs={{0,28},{1,29},{2,30},{3,31},{4,24},{5,25},{6,26},{7,27},{8,0},{9,1... | collective-permute-start | bytes 344072 | tf_op jit(solution)/shard_map/ppermute | solution.py:35
  320.0 26.3 %collective-permute-start.39 = (bf16[288,896]{1,0:T(8,128)(2,1)S(1)}, bf16[288,896]{1,0:T(8,128)(2,1)S(1)}, u32[]{:S(2)}, u32[]{:S(2)}) collective-permute-start(bf16[288,896]{1,0:T(8,128)(2,1)S(1)} %convolution_convert_fusion.11), channel_id=1, source_target_pairs={{0,1},{1,2},{2,3},{3,0},{4,5},{5,6},{6,7},{7,4},{8,9},{9,10},{10,1... | collective-permute-start | bytes 1548296 | tf_op jit(solution)/shard_map/ppermute | solution.py:20
  321.3 26.0 %collective-permute-start.38 = (bf16[288,896]{1,0:T(8,128)(2,1)S(1)}, bf16[288,896]{1,0:T(8,128)(2,1)S(1)}, u32[]{:S(2)}, u32[]{:S(2)}) collective-permute-start(bf16[288,896]{1,0:T(8,128)(2,1)S(1)} %convolution_convert_fusion.8), channel_id=1, source_target_pairs={{0,3},{1,0},{2,1},{3,2},{4,7},{5,4},{6,5},{7,6},{8,11},{9,8},{10,9... | collective-permute-start | bytes 1548296 | tf_op jit(solution)/shard_map/ppermute | solution.py:20
  325.5 20.3 %collective-permute-start.47 = (bf16[288,896]{1,0:T(8,128)(2,1)S(1)}, bf16[288,896]{1,0:T(8,128)(2,1)S(1)}, u32[]{:S(2)}, u32[]{:S(2)}) collective-permute-start(bf16[288,896]{1,0:T(8,128)(2,1)S(1)} %convolution_convert_fusion.10), channel_id=1, source_target_pairs={{0,1},{1,2},{2,3},{3,0},{4,5},{5,6},{6,7},{7,4},{8,9},{9,10},{10,1... | collective-permute-start | bytes 1548296 | tf_op jit(solution)/shard_map/ppermute | solution.py:20
  347.2 80.5 %collective-permute-start.49 = (bf16[288,896]{1,0:T(8,128)(2,1)S(1)}, bf16[288,896]{1,0:T(8,128)(2,1)S(1)}, u32[]{:S(2)}, u32[]{:S(2)}) collective-permute-start(bf16[288,896]{1,0:T(8,128)(2,1)S(1)} %convolution_convert_fusion.18), channel_id=1, source_target_pairs={{0,3},{1,0},{2,1},{3,2},{4,7},{5,4},{6,5},{7,6},{8,11},{9,8},{10,9... | collective-permute-start | bytes 1548296 | tf_op jit(solution)/shard_map/ppermute | solution.py:20
  356.4 74.8 %collective-permute-start.60 = (bf16[288,896]{1,0:T(8,128)(2,1)S(1)}, bf16[288,896]{1,0:T(8,128)(2,1)S(1)}, u32[]{:S(2)}, u32[]{:S(2)}) collective-permute-start(bf16[288,896]{1,0:T(8,128)(2,1)S(1)} %convolution_convert_fusion.16), channel_id=1, source_target_pairs={{0,1},{1,2},{2,3},{3,0},{4,5},{5,6},{6,7},{7,4},{8,9},{9,10},{10,1... | collective-permute-start | bytes 1548296 | tf_op jit(solution)/shard_map/ppermute | solution.py:20
  356.8 74.4 %collective-permute-start.71 = (bf16[288,896]{1,0:T(8,128)(2,1)S(1)}, bf16[288,896]{1,0:T(8,128)(2,1)S(1)}, u32[]{:S(2)}, u32[]{:S(2)}) collective-permute-start(bf16[288,896]{1,0:T(8,128)(2,1)S(1)} %convolution_convert_fusion.14), channel_id=1, source_target_pairs={{0,3},{1,0},{2,1},{3,2},{4,7},{5,4},{6,5},{7,6},{8,11},{9,8},{10,9... | collective-permute-start | bytes 1548296 | tf_op jit(solution)/shard_map/ppermute | solution.py:20
  359.6 21.7 %collective-permute-start.43 = (bf16[288,896]{1,0:T(8,128)(2,1)S(1)}, bf16[288,896]{1,0:T(8,128)(2,1)S(1)}, u32[]{:S(2)}, u32[]{:S(2)}) collective-permute-start(bf16[288,896]{1,0:T(8,128)(2,1)S(1)} %collective-permute-done.42), channel_id=1, source_target_pairs={{0,1},{1,2},{2,3},{3,0},{4,5},{5,6},{6,7},{7,4},{8,9},{9,10},{10,1... | collective-permute-start | bytes 1548296 | tf_op jit(solution)/shard_map/ppermute | solution.py:20
  416.1 18.4 %collective-permute-start.82 = (bf16[288,896]{1,0:T(8,128)(2,1)S(1)}, bf16[288,896]{1,0:T(8,128)(2,1)S(1)}, u32[]{:S(2)}, u32[]{:S(2)}) collective-permute-start(bf16[288,896]{1,0:T(8,128)(2,1)S(1)} %convolution_convert_fusion.12), channel_id=1, source_target_pairs={{0,1},{1,2},{2,3},{3,0},{4,5},{5,6},{6,7},{7,4},{8,9},{9,10},{10,1... | collective-permute-start | bytes 1548296 | tf_op jit(solution)/shard_map/ppermute | solution.py:20
  427.4 57.9 %collective-permute-start.46 = (bf16[288,896]{1,0:T(8,128)(2,1)S(1)}, bf16[288,896]{1,0:T(8,128)(2,1)S(1)}, u32[]{:S(2)}, u32[]{:S(2)}) collective-permute-start(bf16[288,896]{1,0:T(8,128)(2,1)S(1)} %add_convert_fusion.11), channel_id=1, source_target_pairs={{0,1},{1,2},{2,3},{3,0},{4,5},{5,6},{6,7},{7,4},{8,9},{9,10},{10,1... | collective-permute-start | bytes 1548296 | tf_op jit(solution)/shard_map/ppermute | solution.py:20
  427.7 57.5 %collective-permute-start.59 = (bf16[288,896]{1,0:T(8,128)(2,1)S(1)}, bf16[288,896]{1,0:T(8,128)(2,1)S(1)}, u32[]{:S(2)}, u32[]{:S(2)}) collective-permute-start(bf16[288,896]{1,0:T(8,128)(2,1)S(1)} %add_convert_fusion.10), channel_id=1, source_target_pairs={{0,3},{1,0},{2,1},{3,2},{4,7},{5,4},{6,5},{7,6},{8,11},{9,8},{10,9... | collective-permute-start | bytes 1548296 | tf_op jit(solution)/shard_map/ppermute | solution.py:20
  431.2 54.0 %collective-permute-start.70 = (bf16[288,896]{1,0:T(8,128)(2,1)S(1)}, bf16[288,896]{1,0:T(8,128)(2,1)S(1)}, u32[]{:S(2)}, u32[]{:S(2)}) collective-permute-start(bf16[288,896]{1,0:T(8,128)(2,1)S(1)} %add_convert_fusion.9), channel_id=1, source_target_pairs={{0,1},{1,2},{2,3},{3,0},{4,5},{5,6},{6,7},{7,4},{8,9},{9,10},{10,1... | collective-permute-start | bytes 1548296 | tf_op jit(solution)/shard_map/ppermute | solution.py:20
  431.2 54.0 %collective-permute-start.81 = (bf16[288,896]{1,0:T(8,128)(2,1)S(1)}, bf16[288,896]{1,0:T(8,128)(2,1)S(1)}, u32[]{:S(2)}, u32[]{:S(2)}) collective-permute-start(bf16[288,896]{1,0:T(8,128)(2,1)S(1)} %add_convert_fusion.8), channel_id=1, source_target_pairs={{0,3},{1,0},{2,1},{3,2},{4,7},{5,4},{6,5},{7,6},{8,11},{9,8},{10,9... | collective-permute-start | bytes 1548296 | tf_op jit(solution)/shard_map/ppermute | solution.py:20
  434.5 132.6 %collective-permute-start.164 = (bf16[64,3584]{1,0:T(8,128)(2,1)S(1)}, bf16[64,3584]{1,0:T(8,128)(2,1)S(1)}, u32[]{:S(2)}, u32[]{:S(2)}) collective-permute-start(bf16[64,3584]{1,0:T(8,128)(2,1)S(1)} %get-tuple-element.48), channel_id=1, source_target_pairs={{0,224},{32,0},{64,32},{96,64},{128,96},{160,128},{192,160},{224,1... | collective-permute-start | bytes 1376264 | tf_op jit(solution)/shard_map/ppermute | solution.py:40
  511.2 20.8 %collective-permute-start.89 = (bf16[64,896]{1,0:T(8,128)(2,1)S(1)}, bf16[64,896]{1,0:T(8,128)(2,1)S(1)}, u32[]{:S(2)}, u32[]{:S(2)}) collective-permute-start(bf16[64,896]{1,0:T(8,128)(2,1)S(1)} %fusion.49), channel_id=1, source_target_pairs={{0,8},{1,9},{2,10},{3,11},{4,12},{5,13},{6,14},{7,15},{8,16},{9,17... | collective-permute-start | bytes 344072 | tf_op jit(solution)/shard_map/ppermute | solution.py:35
  514.5 21.5 %collective-permute-start.78 = (bf16[64,896]{1,0:T(8,128)(2,1)S(1)}, bf16[64,896]{1,0:T(8,128)(2,1)S(1)}, u32[]{:S(2)}, u32[]{:S(2)}) collective-permute-start(bf16[64,896]{1,0:T(8,128)(2,1)S(1)} %fusion.44), channel_id=1, source_target_pairs={{0,28},{1,29},{2,30},{3,31},{4,24},{5,25},{6,26},{7,27},{8,0},{9,1... | collective-permute-start | bytes 344072 | tf_op jit(solution)/shard_map/ppermute | solution.py:35
  516.6 24.2 %collective-permute-start.67 = (bf16[64,896]{1,0:T(8,128)(2,1)S(1)}, bf16[64,896]{1,0:T(8,128)(2,1)S(1)}, u32[]{:S(2)}, u32[]{:S(2)}) collective-permute-start(bf16[64,896]{1,0:T(8,128)(2,1)S(1)} %fusion.39), channel_id=1, source_target_pairs={{0,8},{1,9},{2,10},{3,11},{4,12},{5,13},{6,14},{7,15},{8,16},{9,17... | collective-permute-start | bytes 344072 | tf_op jit(solution)/shard_map/ppermute | solution.py:35
  532.0 29.4 %collective-permute-start.56 = (bf16[64,896]{1,0:T(8,128)(2,1)S(1)}, bf16[64,896]{1,0:T(8,128)(2,1)S(1)}, u32[]{:S(2)}, u32[]{:S(2)}) collective-permute-start(bf16[64,896]{1,0:T(8,128)(2,1)S(1)} %fusion.34), channel_id=1, source_target_pairs={{0,28},{1,29},{2,30},{3,31},{4,24},{5,25},{6,26},{7,27},{8,0},{9,1... | collective-permute-start | bytes 344072 | tf_op jit(solution)/shard_map/ppermute | solution.py:35
  536.0 25.2 %collective-permute-start.64 = (bf16[64,896]{1,0:T(8,128)(2,1)S(1)}, bf16[64,896]{1,0:T(8,128)(2,1)S(1)}, u32[]{:S(2)}, u32[]{:S(2)}) collective-permute-start(bf16[64,896]{1,0:T(8,128)(2,1)S(1)} %fusion.36), channel_id=1, source_target_pairs={{0,28},{1,29},{2,30},{3,31},{4,24},{5,25},{6,26},{7,27},{8,0},{9,1... | collective-permute-start | bytes 344072 | tf_op jit(solution)/shard_map/ppermute | solution.py:35
  540.6 22.5 %collective-permute-start.53 = (bf16[64,896]{1,0:T(8,128)(2,1)S(1)}, bf16[64,896]{1,0:T(8,128)(2,1)S(1)}, u32[]{:S(2)}, u32[]{:S(2)}) collective-permute-start(bf16[64,896]{1,0:T(8,128)(2,1)S(1)} %fusion.31), channel_id=1, source_target_pairs={{0,8},{1,9},{2,10},{3,11},{4,12},{5,13},{6,14},{7,15},{8,16},{9,17... | collective-permute-start | bytes 344072 | tf_op jit(solution)/shard_map/ppermute | solution.py:35
  540.8 26.3 %collective-permute-start.90 = (bf16[64,896]{1,0:T(8,128)(2,1)S(1)}, bf16[64,896]{1,0:T(8,128)(2,1)S(1)}, u32[]{:S(2)}, u32[]{:S(2)}) collective-permute-start(bf16[64,896]{1,0:T(8,128)(2,1)S(1)} %fusion.27), channel_id=1, source_target_pairs={{0,32},{32,64},{64,96},{96,128},{128,160},{160,192},{192,224},{224... | collective-permute-start | bytes 344072 | tf_op jit(solution)/shard_map/ppermute | solution.py:40
  (133 other events, 1081.0 us)

commit v2 on v1

v2 whole, which is shorter than its diff:
```python
import functools

import jax
import jax.numpy as jnp
from jax import lax
from jax.experimental import pallas as pl
from jax.experimental.pallas import tpu as pltpu
from jax.sharding import PartitionSpec as P

EPSILON = 1e-06
Y_SIZE = 4
LANES = 128
VMEM_BYTES = 24 * 1024 * 1024
CUT_SECOND = (4, 10, 14)
CUT_FIRST = (14, 14)
CUT_END = (7, 7)
CUT_BACK = (14, 14)
CUT_LAST = (8, 8, 6, 6)
BF16 = jnp.bfloat16
F32 = jnp.float32
FEATURES_LAST = (((1,), (1,)), ((), ()))
Z_ORDER = (0, 4, -1, 3, 1, -3, -2, 2)


def shift_y(value, by):
    count = lax.axis_size("local")
    pairs = [(i, i // Y_SIZE * Y_SIZE + (i % Y_SIZE + by) % Y_SIZE) for i in range(count)]
    return lax.ppermute(value, "local", pairs)


def shift_z(value, by):
    nodes = lax.axis_size("node")
    locals_ = lax.axis_size("local")
    depth = nodes * (locals_ // Y_SIZE)
    pairs = []
    for node in range(nodes):
        for place in range(locals_):
            z = (place // Y_SIZE) * nodes + node
            to = (z + by) % depth
            pairs.append(
                (node * locals_ + place, (to % nodes) * locals_ + to // nodes * Y_SIZE + place % Y_SIZE)
            )
    return lax.ppermute(value, ("node", "local"), pairs)


def shift_section(value, by):
    size = lax.axis_size("section")
    return lax.ppermute(value, "section", [(i, (i + by) % size) for i in range(size)])


def hold(value, *marks):
    marks = [mark for mark in marks if mark is not None]
    return lax.optimization_barrier((value, marks))[0] if marks else value


def back(items, count):
    return items[-count] if len(items) >= count else None


def rms_scale(values):
    return lax.rsqrt(jnp.mean(values * values, axis=-1, keepdims=True) + EPSILON)


def cut(width, shares):
    units = width // LANES
    total = sum(shares)
    edges = [round(units * sum(shares[:i]) / total) * LANES for i in range(len(shares) + 1)]
    return list(zip(edges[:-1], edges[1:]))


def tile_of(width):
    units = width // LANES
    return LANES * max(i for i in range(1, 8) if units % i == 0)


def params():
    return pltpu.CompilerParams(vmem_limit_bytes=VMEM_BYTES)


def cost(flops, moved):
    return pl.CostEstimate(flops=flops, bytes_accessed=moved, transcendentals=0)


def opening_kernel(edges, route_f, weight_f, route_b, weight_b, rows, *outs):
    count = rows.shape[0]
    lane = lax.broadcasted_iota(jnp.int32, (count, LANES), 1)
    earlier = (
        lax.broadcasted_iota(jnp.int32, (count, count), 1)
        < lax.broadcasted_iota(jnp.int32, (count, count), 0)
    ).astype(BF16)
    kind = lane // 4
    meta = jnp.zeros((count, LANES), F32)
    for start, route, weight in ((0, route_f, weight_f), (4, route_b, weight_b)):
        first = route[:, 0:1] == lane % 4
        second = route[:, 1:2] == lane % 4
        chosen = jnp.where(first, 1.0, jnp.where(second, 1.0, 0.0))
        before = jnp.dot(earlier, chosen.astype(BF16), preferred_element_type=F32)
        value = jnp.where(first, weight[:, 0:1], jnp.where(second, weight[:, 1:2], 0.0))
        high = value.astype(BF16).astype(F32)
        middle = (value - high).astype(BF16).astype(F32)
        low = value - high - middle
        meta = jnp.where(kind == start, jnp.where(chosen > 0.0, before, -1.0), meta)
        meta = jnp.where(kind == start + 1, high, meta)
        meta = jnp.where(kind == start + 2, middle, meta)
        meta = jnp.where(kind == start + 3, low, meta)
    for i, ((low_edge, high_edge), out) in enumerate(zip(edges, outs)):
        span = high_edge - low_edge
        out[:, :span] = rows[:, low_edge:high_edge]
        if i == 0:
            out[:, span:] = meta.astype(BF16)


def opening(edges, route_f, weight_f, route_b, weight_b, rows):
    count = rows.shape[0]
    shapes = [
        jax.ShapeDtypeStruct((count, high - low + (LANES if i == 0 else 0)), BF16)
        for i, (low, high) in enumerate(edges)
    ]
    return pl.pallas_call(
        functools.partial(opening_kernel, edges),
        out_shape=shapes,
        compiler_params=params(),
        cost_estimate=cost(0, 4 * rows.size),
    )(route_f, weight_f, route_b, weight_b, rows)


def norm_kernel(edges, rows, gain, *outs):
    values = rows[...].astype(F32)
    normed = (values * rms_scale(values) * gain[...]).astype(BF16)
    for (low, high), out in zip(edges, outs):
        out[...] = normed[:, low:high]


def norm(edges, rows, gain):
    return pl.pallas_call(
        functools.partial(norm_kernel, edges),
        out_shape=[
            jax.ShapeDtypeStruct((rows.shape[0], high - low), BF16) for low, high in edges
        ],
        compiler_params=params(),
        cost_estimate=cost(8 * rows.size, 4 * rows.size),
    )(rows, gain)


def tables_kernel(capacity, slots, expert, z_of, *refs):
    blocks, outs = refs[:8], refs[8:]
    metas = jnp.concatenate([ref[...].astype(F32) for ref in blocks], axis=0)
    count = metas.shape[0]
    lane = lax.broadcasted_iota(jnp.int32, metas.shape, 1)
    mine = lane % 4 == expert[...]
    kind = lane // 4
    padded = outs[0].shape[0] // LANES * LANES + (LANES if outs[0].shape[0] % LANES else 0)
    places = lax.broadcasted_iota(jnp.int32, (count, padded), 1)
    for i, start in enumerate((0, 4)):
        slot = jnp.sum(jnp.where(mine & (kind == start), metas, 0.0), axis=1, keepdims=True)
        high = mine & (kind > start) & (kind < start + 4)
        weight = jnp.sum(jnp.where(high, metas, 0.0), axis=1, keepdims=True)
        target = jnp.where(slot >= 0.0, z_of[...] * capacity + slot.astype(jnp.int32), -1)
        down = jnp.where(target == places, 1.0, 0.0)
        across, down_out, weight_out = outs[3 * i : 3 * i + 3]
        down_out[...] = down[:, :slots].astype(BF16)
        across[...] = down.T[:slots].astype(BF16)
        weight_out[...] = jnp.sum((down * weight).T, axis=1, keepdims=True)[:slots]


def tables(expert, z_of, blocks, row, column, capacity):
    count = z_of.shape[0]
    slots = capacity * len(blocks)
    step = count // len(blocks)
    one = [
        jax.ShapeDtypeStruct((slots, count), BF16),
        jax.ShapeDtypeStruct((count, slots), BF16),
        jax.ShapeDtypeStruct((slots, 1), F32),
    ]
    whole = lambda shape: pl.BlockSpec(shape, lambda i: (0, 0))
    return pl.pallas_call(
        functools.partial(tables_kernel, capacity, slots),
        grid=(1,),
        out_shape=one * 2,
        in_specs=[whole((1, LANES)), whole((count, 1))]
        + [pl.BlockSpec((step, LANES), lambda i: (row, column))] * len(blocks),
        out_specs=[whole(item.shape) for item in one * 2],
        compiler_params=params(),
        cost_estimate=cost(0, 8 * slots * count),
    )(expert, z_of, *blocks)


def select_kernel(table, scale, *refs):
    blocks, out = refs[:-1], refs[-1]
    values = jnp.concatenate([ref[...] for ref in blocks], axis=0)
    total = jnp.dot(table[...], values, preferred_element_type=F32)
    out[...] = (total * scale[...]).astype(BF16)


def select(table, scale, blocks, width, row=0, column=0):
    rows, tokens = table.shape
    tile = tile_of(width)
    step = tokens // len(blocks)
    return pl.pallas_call(
        select_kernel,
        grid=(width // tile,),
        out_shape=jax.ShapeDtypeStruct((rows, width), BF16),
        in_specs=[
            pl.BlockSpec((rows, tokens), lambda i: (0, 0)),
            pl.BlockSpec((rows, 1), lambda i: (0, 0)),
        ]
        + [pl.BlockSpec((step, tile), lambda i: (row, i + column // tile))] * len(blocks),
        out_specs=pl.BlockSpec((rows, tile), lambda i: (0, i)),
        compiler_params=params(),
        cost_estimate=cost(2 * rows * tokens * width, 2 * (rows + tokens) * width),
    )(table, scale, *blocks)


def spread_kernel(table, scale, rows, *outs):
    values = (rows[...] * scale[...]).astype(BF16)
    total = jnp.dot(table[...], values, preferred_element_type=F32).astype(BF16)
    step = table.shape[0] // len(outs)
    for i, ref in enumerate(outs):
        ref[...] = total[i * step : (i + 1) * step]


def spread(table, scale, rows, count):
    tokens, slots = table.shape
    width = rows.shape[1]
    tile = tile_of(width)
    return pl.pallas_call(
        spread_kernel,
        grid=(width // tile,),
        out_shape=[jax.ShapeDtypeStruct((tokens // count, width), BF16)] * count,
        in_specs=[
            pl.BlockSpec((tokens, slots), lambda i: (0, 0)),
            pl.BlockSpec((slots, 1), lambda i: (0, 0)),
            pl.BlockSpec((slots, tile), lambda i: (0, i)),
        ],
        out_specs=[pl.BlockSpec((tokens // count, tile), lambda i: (0, i))] * count,
        compiler_params=params(),
        cost_estimate=cost(2 * slots * tokens * width, (4 * slots + 2 * tokens) * width),
    )(table, scale, rows)


def local(
    x_fwd,
    route_fwd,
    weight_fwd,
    x_bwd,
    grad_out,
    route_bwd,
    weight_bwd,
    saved_pre,
    norm_gain,
    w_gate,
    w_up,
    w_down,
):
    experts = lax.axis_size("node")
    halves = lax.axis_size("local") // Y_SIZE
    depth = experts * halves
    tokens, width = x_fwd.shape[1:]
    units = w_gate.shape[3]
    capacity = saved_pre.shape[2] // (depth * Y_SIZE)
    group = depth * capacity
    expert = lax.axis_index("node")
    place = lax.axis_index("local")
    my_y = place % Y_SIZE
    my_z = place // Y_SIZE * experts + expert
    gain = norm_gain[0]
    upstream = grad_out[0]

    def columns(value, edge):
        return value[:, edge[0] : edge[1]]

    cuts_second = cut(width, CUT_SECOND)
    cuts_first = cut(width, CUT_FIRST)
    cuts_back = cut(width, CUT_BACK)
    cuts_last = cut(width, CUT_LAST)
    blocks = opening(
        cuts_second, route_fwd[0], weight_fwd[0], route_bwd[0], weight_bwd[0], upstream
    )
    expert_row = jnp.full((1, LANES), expert, jnp.int32)
    z_of = jnp.concatenate(
        [jnp.full((tokens, 1), (my_z + i + depth) % depth, jnp.int32) for i in Z_ORDER], axis=0
    )
    ones = jnp.ones((group, 1), F32)

    firsts, thirds, starts, turns = [], [], [], []

    def open_z(block):
        block = hold(block, back(firsts, 1), back(starts, 2))
        got = {0: block, -1: shift_z(block, 1), 1: shift_z(block, -1)}
        firsts.append((got[-1], got[1]))
        return got

    def close_z(got, flip, *marks):
        got[-1], got[1] = hold((got[-1], got[1]), back(thirds, 1))
        for step in range(2, 5):
            if step == 3:
                got[-2], got[2] = hold((got[-2], got[2]), *marks)
            if step == 4:
                got[-3], got[3] = hold((got[-3], got[3]), firsts[-1])
            if step < 4 or not flip:
                got[-step] = shift_z(got[1 - step], 1)
            if step < 4 or flip:
                got[step] = shift_z(got[step - 1], -1)
        thirds.append((got[-3], got[3]))
        got[4] = got[4] if flip else got[-4]
        return [got[i] for i in Z_ORDER]

    def gather_y(block, *marks):
        block = hold(block, back(starts, 2), back(turns, 2), *marks)
        before = shift_y(block, 1)
        after = shift_y(block, -1)
        starts.append((before, after))
        return block, before, after

    def finish_y(parts, flip, *marks):
        block, before, after = parts
        first = hold(after if flip else before, *marks)
        far = shift_y(first, -1 if flip else 1)
        turns.append(far)
        return {0: block, -1: before, 1: after, 2: far}

    block = blocks[0]
    direct = [block if i == 0 else shift_z(block, -i) for i in Z_ORDER]
    firsts.append((direct[2], direct[4]))
    x_first = x_fwd[0]
    blocks += norm(cuts_first, hold(x_first, direct[2]), gain.reshape(1, width))
    across_first, down_first, weight_first, across_second, down_second, weight_second = tables(
        expert_row, z_of, direct, 0, cuts_second[0][1] // LANES, capacity
    )

    count_second = len(cuts_second)
    arrived, opened = [], None
    for c, (low, high) in enumerate(cuts_second + cuts_first[:1]):
        flip = c % 2 == 1
        upcoming = open_z(blocks[c + 1])
        parts = close_z(opened, flip, starts[0] if c == 1 else None) if c else direct
        opened = upcoming
        if c < count_second:
            rows = select(across_second, weight_second, parts, high - low)
        else:
            rows = select(across_first, ones, parts, high - low)
        parts = gather_y(rows, None if c else firsts[-1])
        arrived.append(finish_y(parts, flip))
    parts_last = close_z(opened, count_second % 2 == 0)

    gate_w, up_w, down_w, stored_all = hold(
        (w_gate[0, 0], w_up[0, 0], w_down[0, 0], saved_pre[0, 0]), starts[1]
    )
    both_w = jnp.concatenate([gate_w, up_w], axis=1)
    saved = stored_all.reshape(halves, Y_SIZE, experts * capacity, 2, units)
    pre_grads = {}
    for r in (2, 1, -1, 0):
        hidden_grad = sum(
            lax.dot_general(
                parts[r], columns(down_w, edge), FEATURES_LAST, preferred_element_type=F32
            )
            for parts, edge in zip(arrived, cuts_second)
        )
        stored = lax.dynamic_index_in_dim(
            saved, (my_y + r + Y_SIZE) % Y_SIZE, 1, keepdims=False
        ).reshape(group, 2, units)
        gate = stored[:, 0, :].astype(F32)
        upper = stored[:, 1, :].astype(F32)
        sigma = jax.nn.sigmoid(gate)
        grad_gate = hidden_grad * upper * sigma * (1.0 + gate * (1.0 - sigma))
        grad_upper = hidden_grad * gate * sigma
        pre_grads[r] = jnp.concatenate([grad_gate, grad_upper], axis=1).astype(BF16)

    def second_term(edge, r):
        return lax.dot_general(
            pre_grads[r], both_w[edge[0] : edge[1]], FEATURES_LAST, preferred_element_type=F32
        )

    def first_term(edge, r):
        return jnp.dot(hidden[r], columns(down_w, edge), preferred_element_type=F32)

    def start_back(term, edge, side, *marks):
        far, straight = hold((term(edge, 2).astype(BF16), term(edge, -side).astype(BF16)), *marks)
        return shift_y(far, side), shift_y(straight, -side)

    def through_back(term, edge, side, far, straight):
        return shift_y((term(edge, side) + far.astype(F32)).astype(BF16), side)

    def end_back(term, edge, side, far, straight, through):
        return term(edge, 0) + through.astype(F32) + straight.astype(F32)

    def scatter_z(parts, flip, *waits):
        parts = dict(zip(Z_ORDER, parts))
        side = 1 if flip else -1
        long, short = parts[4], parts[-side * 3]
        marks = []
        for step in (3, 2, 1, 0):
            if 3 - step < len(waits):
                long, short = hold((long, short), *waits[3 - step])
            long = shift_z(long, side)
            if step < 3:
                short = shift_z(short, -side)
            marks.append((long, short))
            if step:
                long = (parts[side * step].astype(F32) + long.astype(F32)).astype(BF16)
            if 0 < step < 3:
                short = (parts[-side * step].astype(F32) + short.astype(F32)).astype(BF16)
        return parts[0].astype(F32) + long.astype(F32) + short.astype(F32), marks

    ways = (1, -1, 1, -1)
    begun = [start_back(second_term, *item) for item in zip(cuts_back, ways)]
    turned = [through_back(second_term, *item, *got) for *item, got in zip(cuts_back, ways, begun)]
    rows = [
        end_back(second_term, *item, *got, through)
        for *item, got, through in zip(cuts_back, ways, begun, turned)
    ]
    edges_first = cuts_first[:1] + cut(width - cuts_first[1][0], CUT_END)
    edges_first[1:] = [(low + cuts_first[1][0], high + cuts_first[1][0]) for low, high in edges_first[1:]]
    pending = []
    for i, (low, high) in enumerate(edges_first[1:]):
        rows_first = select(across_first, ones, parts_last, high - low, 0, low - cuts_first[1][0])
        rows_first = hold(rows_first, begun[i])
        pending.append((rows_first, shift_y(rows_first, 1), shift_y(rows_first, -1)))

    arrived.append(finish_y(pending[0], False))
    arrived.append(finish_y(pending[1], True))
    hidden = {}
    for r in (2, 1, -1, 0):
        both = sum(
            jnp.dot(parts[r], both_w[edge[0] : edge[1]], preferred_element_type=F32)
            for parts, edge in zip(arrived[count_second:], edges_first)
        )
        hidden[r] = (jax.nn.silu(both[:, :units]) * both[:, units:]).astype(BF16)

    opened = [
        start_back(first_term, edge, side, turned) for edge, side in zip(cuts_last[:2], ways)
    ]
    parts = spread(down_second, ones, jnp.concatenate(rows, axis=1), depth)
    normed_grad, ring = scatter_z(parts, False, [], [], [opened])
    opened += [
        start_back(first_term, edge, side, ring[0]) for edge, side in zip(cuts_last[2:], ways)
    ]

    x_second = x_bwd[0].astype(F32)
    scale = rms_scale(x_second)
    along = gain * normed_grad
    input_grad = (
        upstream.astype(F32)
        + scale * along
        - x_second * (scale * scale * scale) * jnp.mean(along * x_second, axis=-1, keepdims=True)
    ).astype(BF16)
    grad_prev = shift_section(input_grad, -1)

    act_next = []
    turned = [through_back(first_term, *item, *got) for *item, got in zip(cuts_last, ways, opened)]
    rows = [
        end_back(first_term, *item, *got, through)
        for *item, got, through in zip(cuts_last, ways, opened, turned)
    ]
    for step in range(2):
        pair = jnp.concatenate(rows[2 * step : 2 * step + 2], axis=1)
        edge = (cuts_last[2 * step][0], cuts_last[2 * step + 1][1])
        added, _ = scatter_z(spread(down_first, weight_first, pair, depth), step % 2 == 0)
        mixed = columns(x_first, edge).astype(F32) + added
        act_next.append(shift_section(mixed.astype(BF16), 1))
    return (jnp.concatenate(act_next, axis=1)[None], grad_prev[None])


def solution(mesh):
    tokens = P("section", ("node", "local"), None)
    in_specs = (
        tokens,
        tokens,
        tokens,
        tokens,
        tokens,
        tokens,
        tokens,
        P("section", "node", None, None, "local"),
        P("section", None),
        P("section", "node", None, "local"),
        P("section", "node", None, "local"),
        P("section", "node", "local", None),
    )
    return jax.shard_map(
        local, mesh=mesh, in_specs=in_specs, out_specs=(tokens, tokens), check_vma=False
    )
```

time: 580 us -> 427 us (0.74)
  the two profiles are of different devices: /device:TPU:1 before, /device:TPU:24 now
where the time goes in v2:
time: 427 us; the launch traced here: 419 us
  waiting for transfers between devices  221 us (52%)
  starting transfers between devices  131 us (31%)
  matrix products  25.9 us (6%)
  local copies, waits for them, and re-layouts  17.6 us (4%)
  Pallas kernels  15.9 us (4%)
  other arithmetic  5.15 us (1%)
    ppermute x36, waiting for transfers between devices, shift_y(): return lax.ppermute(value, 'local', pairs)  144 us
    ppermute x56, starting transfers between devices, shift_z(): return lax.ppermute(value, ('node', 'local'), pairs)  84.3 us
    ppermute x56, waiting for transfers between devices, shift_z(): return lax.ppermute(value, ('node', 'local'), pairs)  69.5 us
    ppermute x36, starting transfers between devices, shift_y(): return lax.ppermute(value, 'local', pairs)  45.1 us
    unnamed x64, local copies, waits for them, and re-layouts  13.1 us
    dot_general x12, matrix products, local(): lax.dot_general(parts[r], columns(down_w, edge), FEATURES_LAST, preferred...  8.86 us
  transfers between devices with their start and end apart: 95, of which 40 were waited for; matrix products, arithmetic and copies ran while one was open for 7% of the time, Pallas kernels for 3%

profile of v2, /device:TPU:24, one launch (start us, length us, event | category | flops | bytes accessed | tf_op | source)
XLA Modules:
  0.0 419.2 jit_solution(3511110424529927167)
XLA Ops:
  5.0 5.9 %collective-permute-start.3 = (bf16[64,640]{1,0:T(8,128)(2,1)S(1)}, bf16[64,640]{1,0:T(8,128)(2,1)S(1)}, u32[]{:S(2)}, u32[]{:S(2)}) collective-permute-start(bf16[64,640]{1,0:T(8,128)(2,1)S(1)} %get-tuple-element.77.refs_0_), channel_id=1, source_target_pairs={{0,28},{1,29},{2,30},{3,31},{4,24},{5,25},{6,26},{7,27},{8,0},{9,1... | collective-permute-start | bytes 245768 | tf_op jit(solution)/shard_map/ppermute | solution.py:43
  11.0 2.5 collective-permute-start.6
  13.9 2.7 collective-permute-done.1.refs_2_
  20.4 3.3 collective-permute-start.2
  28.5 4.3 %collective-permute-done.refs_1_ = bf16[64,640]{1,0:T(8,128)(2,1)S(1)} collective-permute-done((bf16[64,640]{1,0:T(8,128)(2,1)S(1)}, bf16[64,640]{1,0:T(8,128)(2,1)S(1)}, u32[]{:S(2)}, u32[]{:S(2)}) %collective-permute-start) | collective-permute-done | bytes 81952 | tf_op jit(solution)/shard_map/ppermute | solution.py:43
  35.3 2.5 collective-permute-start.11
  39.8 3.6 collective-permute-start.10
  45.3 2.9 collective-permute-done.15.refs_6_
  48.2 3.2 collective-permute-start.18
  52.3 2.4 collective-permute-done.17.refs_5_
  56.1 3.7 collective-permute-start.27
  65.3 3.2 collective-permute-start.28
  75.9 3.5 collective-permute-done.20.refs_5_
  84.2 3.1 collective-permute-done.40.refs_1_
  100.0 3.2 collective-permute-start.26
  105.5 4.1 collective-permute-done.24.refs_5_
  109.5 3.3 collective-permute-start.41
  114.2 3.3 collective-permute-start.32
  117.5 3.4 collective-permute-done.34.refs_6_
  124.2 2.7 collective-permute-done.36.refs_7_
  139.5 3.3 collective-permute-start.42
  148.5 17.5 %collective-permute-done.42 = bf16[288,1792]{1,0:T(8,128)(2,1)S(1)} collective-permute-done((bf16[288,1792]{1,0:T(8,128)(2,1)S(1)}, bf16[288,1792]{1,0:T(8,128)(2,1)S(1)}, u32[]{:S(2)}, u32[]{:S(2)}) %collective-permute-start.42) | collective-permute-done | bytes 1032224 | tf_op jit(solution)/shard_map/ppermute | solution.py:28
  177.5 10.7 %collective-permute-done.47 = bf16[288,1792]{1,0:T(8,128)(2,1)S(1)} collective-permute-done((bf16[288,1792]{1,0:T(8,128)(2,1)S(1)}, bf16[288,1792]{1,0:T(8,128)(2,1)S(1)}, u32[]{:S(2)}, u32[]{:S(2)}) %collective-permute-start.47) | collective-permute-done | bytes 1032224 | tf_op jit(solution)/shard_map/ppermute | solution.py:28
  190.2 19.5 %collective-permute-done.45 = bf16[288,1792]{1,0:T(8,128)(2,1)S(1)} collective-permute-done((bf16[288,1792]{1,0:T(8,128)(2,1)S(1)}, bf16[288,1792]{1,0:T(8,128)(2,1)S(1)}, u32[]{:S(2)}, u32[]{:S(2)}) %collective-permute-start.45) | collective-permute-done | bytes 1032224 | tf_op jit(solution)/shard_map/ppermute | solution.py:28
  215.2 24.2 %collective-permute-done.50 = bf16[288,896]{1,0:T(8,128)(2,1)S(1)} collective-permute-done((bf16[288,896]{1,0:T(8,128)(2,1)S(1)}, bf16[288,896]{1,0:T(8,128)(2,1)S(1)}, u32[]{:S(2)}, u32[]{:S(2)}) %collective-permute-start.50) | collective-permute-done | bytes 516128 | tf_op jit(solution)/shard_map/ppermute | solution.py:28
  239.9 10.2 %collective-permute-done.49 = bf16[288,896]{1,0:T(8,128)(2,1)S(1)} collective-permute-done((bf16[288,896]{1,0:T(8,128)(2,1)S(1)}, bf16[288,896]{1,0:T(8,128)(2,1)S(1)}, u32[]{:S(2)}, u32[]{:S(2)}) %collective-permute-start.49) | collective-permute-done | bytes 516128 | tf_op jit(solution)/shard_map/ppermute | solution.py:28
  251.6 3.3 collective-permute-start.57
  257.1 3.5 collective-permute-start.53
  261.2 16.9 %collective-permute-done.54 = bf16[288,896]{1,0:T(8,128)(2,1)S(1)} collective-permute-done((bf16[288,896]{1,0:T(8,128)(2,1)S(1)}, bf16[288,896]{1,0:T(8,128)(2,1)S(1)}, u32[]{:S(2)}, u32[]{:S(2)}) %collective-permute-start.54) | collective-permute-done | bytes 516128 | tf_op jit(solution)/shard_map/ppermute | solution.py:28
  283.2 3.6 shard_map.141
  288.8 3.7 collective-permute-start.59
  295.3 3.7 collective-permute-start.64
  300.7 5.1 %collective-permute-done.59 = bf16[288,1024]{1,0:T(8,128)(2,1)S(1)} collective-permute-done((bf16[288,1024]{1,0:T(8,128)(2,1)S(1)}, bf16[288,1024]{1,0:T(8,128)(2,1)S(1)}, u32[]{:S(2)}, u32[]{:S(2)}) %collective-permute-start.59) | collective-permute-done | bytes 589856 | tf_op jit(solution)/shard_map/ppermute | solution.py:28
  306.1 14.1 %collective-permute-done.62 = bf16[288,1024]{1,0:T(8,128)(2,1)S(1)} collective-permute-done((bf16[288,1024]{1,0:T(8,128)(2,1)S(1)}, bf16[288,1024]{1,0:T(8,128)(2,1)S(1)}, u32[]{:S(2)}, u32[]{:S(2)}) %collective-permute-start.62) | collective-permute-done | bytes 589856 | tf_op jit(solution)/shard_map/ppermute | solution.py:28
  323.2 14.1 %collective-permute-done.77 = bf16[288,768]{1,0:T(8,128)(2,1)S(1)} collective-permute-done((bf16[288,768]{1,0:T(8,128)(2,1)S(1)}, bf16[288,768]{1,0:T(8,128)(2,1)S(1)}, u32[]{:S(2)}, u32[]{:S(2)}) %collective-permute-start.77) | collective-permute-done | bytes 442400 | tf_op jit(solution)/shard_map/ppermute | solution.py:28
  341.2 6.0 %collective-permute-done.60 = bf16[288,1024]{1,0:T(8,128)(2,1)S(1)} collective-permute-done((bf16[288,1024]{1,0:T(8,128)(2,1)S(1)}, bf16[288,1024]{1,0:T(8,128)(2,1)S(1)}, u32[]{:S(2)}, u32[]{:S(2)}) %collective-permute-start.60) | collective-permute-done | bytes 589856 | tf_op jit(solution)/shard_map/ppermute | solution.py:28
  350.9 2.4 shard_map.140
  353.8 2.8 collective-permute-done.75
  356.9 3.3 collective-permute-start.69
  364.6 3.4 collective-permute-done.92
  368.1 2.9 collective-permute-done.65
  371.6 3.3 collective-permute-start.70
  377.1 10.8 %collective-permute-done.66 = bf16[64,2048]{1,0:T(8,128)(2,1)S(1)} collective-permute-done((bf16[64,2048]{1,0:T(8,128)(2,1)S(1)}, bf16[64,2048]{1,0:T(8,128)(2,1)S(1)}, u32[]{:S(2)}, u32[]{:S(2)}) %collective-permute-start.66) | collective-permute-done | bytes 262176 | tf_op jit(solution)/shard_map/ppermute | solution.py:43
  388.2 3.3 collective-permute-start.71
  391.5 3.3 collective-permute-done.85
  398.1 2.4 collective-permute-done.82
  401.8 6.1 %collective-permute-done.68 = bf16[64,2048]{1,0:T(8,128)(2,1)S(1)} collective-permute-done((bf16[64,2048]{1,0:T(8,128)(2,1)S(1)}, bf16[64,2048]{1,0:T(8,128)(2,1)S(1)}, u32[]{:S(2)}, u32[]{:S(2)}) %collective-permute-start.68) | collective-permute-done | bytes 262176 | tf_op jit(solution)/shard_map/ppermute | solution.py:43
  409.9 7.3 %collective-permute-done.87 = bf16[64,1536]{1,0:T(8,128)(2,1)S(1)} collective-permute-done((bf16[64,1536]{1,0:T(8,128)(2,1)S(1)}, bf16[64,1536]{1,0:T(8,128)(2,1)S(1)}, u32[]{:S(2)}, u32[]{:S(2)}) %collective-permute-start.87) | collective-permute-done | bytes 196640 | tf_op jit(solution)/shard_map/ppermute | solution.py:48
  (313 shorter events, 139.4 us)
Async XLA Ops:
  16.6 17.8 %collective-permute-start.8 = (bf16[64,1280]{1,0:T(8,128)(2,1)S(1)}, bf16[64,1280]{1,0:T(8,128)(2,1)}, u32[]{:S(2)}, u32[]{:S(2)}) collective-permute-start(bf16[64,1280]{1,0:T(8,128)(2,1)S(1)} %get-tuple-element.85.refs_0_), channel_id=1, source_target_pairs={{0,28},{1,29},{2,30},{3,31},{4,24},{5,25},{6,26},{7,27},{8,0},{9,1... | collective-permute-start | bytes 491528 | tf_op jit(solution)/shard_map/ppermute | solution.py:43
  18.4 16.1 %collective-permute-start.7 = (bf16[64,1280]{1,0:T(8,128)(2,1)S(1)}, bf16[64,1280]{1,0:T(8,128)(2,1)}, u32[]{:S(2)}, u32[]{:S(2)}) collective-permute-start(bf16[64,1280]{1,0:T(8,128)(2,1)S(1)} %get-tuple-element.85.refs_0_), channel_id=1, source_target_pairs={{0,8},{1,9},{2,10},{3,11},{4,12},{5,13},{6,14},{7,15},{8,16},{9,17... | collective-permute-start | bytes 491528 | tf_op jit(solution)/shard_map/ppermute | solution.py:43
  34.4 13.7 %collective-permute-start.12 = (bf16[288,512]{1,0:T(8,128)(2,1)S(1)}, bf16[288,512]{1,0:T(8,128)(2,1)S(1)}, u32[]{:S(2)}, u32[]{:S(2)}) collective-permute-start(bf16[288,512]{1,0:T(8,128)(2,1)S(1)} %shard_map.134), channel_id=1, source_target_pairs={{0,3},{1,0},{2,1},{3,2},{4,7},{5,4},{6,5},{7,6},{8,11},{9,8},{10,9... | collective-permute-start | bytes 884744 | tf_op jit(solution)/shard_map/ppermute | solution.py:28
  65.2 38.0 %collective-permute-start.29 = (bf16[288,1280]{1,0:T(8,128)(2,1)S(1)}, bf16[288,1280]{1,0:T(8,128)(2,1)}, u32[]{:S(2)}, u32[]{:S(2)}) collective-permute-start(bf16[288,1280]{1,0:T(8,128)(2,1)S(1)} %shard_map.135), channel_id=1, source_target_pairs={{0,3},{1,0},{2,1},{3,2},{4,7},{5,4},{6,5},{7,6},{8,11},{9,8},{10,9... | collective-permute-start | bytes 2211848 | tf_op jit(solution)/shard_map/ppermute | solution.py:28
  65.3 37.9 %collective-permute-start.28 = (bf16[288,1280]{1,0:T(8,128)(2,1)S(1)}, bf16[288,1280]{1,0:T(8,128)(2,1)}, u32[]{:S(2)}, u32[]{:S(2)}) collective-permute-start(bf16[288,1280]{1,0:T(8,128)(2,1)S(1)} %shard_map.135), channel_id=1, source_target_pairs={{0,1},{1,2},{2,3},{3,0},{4,5},{5,6},{6,7},{7,4},{8,9},{9,10},{10,1... | collective-permute-start | bytes 2211848 | tf_op jit(solution)/shard_map/ppermute | solution.py:28
  82.0 17.9 %collective-permute-start.39 = (bf16[288,512]{1,0:T(8,128)(2,1)}, bf16[288,512]{1,0:T(8,128)(2,1)}, u32[]{:S(2)}, u32[]{:S(2)}) collective-permute-start(bf16[288,512]{1,0:T(8,128)(2,1)} %collective-permute-done.11), channel_id=1, source_target_pairs={{0,1},{1,2},{2,3},{3,0},{4,5},{5,6},{6,7},{7,4},{8,9},{9,10},{10,1... | collective-permute-start | bytes 884744 | tf_op jit(solution)/shard_map/ppermute | solution.py:28
  82.0 17.9 %collective-permute-start.23 = (bf16[64,1792]{1,0:T(8,128)(2,1)}, bf16[64,1792]{1,0:T(8,128)(2,1)}, u32[]{:S(2)}, u32[]{:S(2)}) collective-permute-start(bf16[64,1792]{1,0:T(8,128)(2,1)} %collective-permute-done.13.refs_2_), channel_id=1, source_target_pairs={{0,8},{1,9},{2,10},{3,11},{4,12},{5,13},{6,14},{7,15},{8,16},{9,17... | collective-permute-start | bytes 688136 | tf_op jit(solution)/shard_map/ppermute | solution.py:43
  99.8 39.1 %collective-permute-start.46 = (bf16[288,1792]{1,0:T(8,128)(2,1)S(1)}, bf16[288,1792]{1,0:T(8,128)(2,1)S(1)}, u32[]{:S(2)}, u32[]{:S(2)}) collective-permute-start(bf16[288,1792]{1,0:T(8,128)(2,1)S(1)} %shard_map.138), channel_id=1, source_target_pairs={{0,3},{1,0},{2,1},{3,2},{4,7},{5,4},{6,5},{7,6},{8,11},{9,8},{10,9... | collective-permute-start | bytes 3096584 | tf_op jit(solution)/shard_map/ppermute | solution.py:28
  109.5 29.9 %collective-permute-start.41 = (bf16[288,1792]{1,0:T(8,128)(2,1)S(1)}, bf16[288,1792]{1,0:T(8,128)(2,1)S(1)}, u32[]{:S(2)}, u32[]{:S(2)}) collective-permute-start(bf16[288,1792]{1,0:T(8,128)(2,1)S(1)} %shard_map.138), channel_id=1, source_target_pairs={{0,1},{1,2},{2,3},{3,0},{4,5},{5,6},{6,7},{7,4},{8,9},{9,10},{10,1... | collective-permute-start | bytes 3096584 | tf_op jit(solution)/shard_map/ppermute | solution.py:28
  112.9 25.7 %collective-permute-start.33 = (bf16[288,1280]{1,0:T(8,128)(2,1)}, bf16[288,1280]{1,0:T(8,128)(2,1)S(1)}, u32[]{:S(2)}, u32[]{:S(2)}) collective-permute-start(bf16[288,1280]{1,0:T(8,128)(2,1)} %collective-permute-done.29), channel_id=1, source_target_pairs={{0,3},{1,0},{2,1},{3,2},{4,7},{5,4},{6,5},{7,6},{8,11},{9,8},{10,9... | collective-permute-start | bytes 2211848 | tf_op jit(solution)/shard_map/ppermute | solution.py:28
  114.2 14.5 %collective-permute-start.32 = (bf16[64,1792]{1,0:T(8,128)(2,1)S(1)}, bf16[64,1792]{1,0:T(8,128)(2,1)S(1)}, u32[]{:S(2)}, u32[]{:S(2)}) collective-permute-start(bf16[64,1792]{1,0:T(8,128)(2,1)S(1)} %collective-permute-done.26.refs_3_), channel_id=1, source_target_pairs={{0,28},{1,29},{2,30},{3,31},{4,24},{5,25},{6,26},{7,27},{8,0},{9,1... | collective-permute-start | bytes 688136 | tf_op jit(solution)/shard_map/ppermute | solution.py:43
  135.0 36.0 %collective-permute-start.38 = (bf16[64,1792]{1,0:T(8,128)(2,1)S(1)}, bf16[64,1792]{1,0:T(8,128)(2,1)S(1)}, u32[]{:S(2)}, u32[]{:S(2)}) collective-permute-start(bf16[64,1792]{1,0:T(8,128)(2,1)S(1)} %collective-permute-done.35.refs_5_), channel_id=1, source_target_pairs={{0,8},{1,9},{2,10},{3,11},{4,12},{5,13},{6,14},{7,15},{8,16},{9,17... | collective-permute-start | bytes 688136 | tf_op jit(solution)/shard_map/ppermute | solution.py:43
  138.6 36.8 %collective-permute-start.48 = (bf16[288,1792]{1,0:T(8,128)(2,1)S(1)}, bf16[288,1792]{1,0:T(8,128)(2,1)S(1)}, u32[]{:S(2)}, u32[]{:S(2)}) collective-permute-start(bf16[288,1792]{1,0:T(8,128)(2,1)S(1)} %shard_map.136), channel_id=1, source_target_pairs={{0,3},{1,0},{2,1},{3,2},{4,7},{5,4},{6,5},{7,6},{8,11},{9,8},{10,9... | collective-permute-start | bytes 3096584 | tf_op jit(solution)/shard_map/ppermute | solution.py:28
  139.5 26.6 %collective-permute-start.42 = (bf16[288,1792]{1,0:T(8,128)(2,1)S(1)}, bf16[288,1792]{1,0:T(8,128)(2,1)S(1)}, u32[]{:S(2)}, u32[]{:S(2)}) collective-permute-start(bf16[288,1792]{1,0:T(8,128)(2,1)S(1)} %collective-permute-done.41), channel_id=1, source_target_pairs={{0,1},{1,2},{2,3},{3,0},{4,5},{5,6},{6,7},{7,4},{8,9},{9,10},{10,1... | collective-permute-start | bytes 3096584 | tf_op jit(solution)/shard_map/ppermute | solution.py:28
  143.8 44.3 %collective-permute-start.47 = (bf16[288,1792]{1,0:T(8,128)(2,1)S(1)}, bf16[288,1792]{1,0:T(8,128)(2,1)S(1)}, u32[]{:S(2)}, u32[]{:S(2)}) collective-permute-start(bf16[288,1792]{1,0:T(8,128)(2,1)S(1)} %convolution_convert_fusion), channel_id=1, source_target_pairs={{0,1},{1,2},{2,3},{3,0},{4,5},{5,6},{6,7},{7,4},{8,9},{9,10},{10,1... | collective-permute-start | bytes 3096584 | tf_op jit(solution)/shard_map/ppermute | solution.py:28
  148.2 63.8 %collective-permute-start.44 = (bf16[288,1792]{1,0:T(8,128)(2,1)S(1)}, bf16[288,1792]{1,0:T(8,128)(2,1)S(1)}, u32[]{:S(2)}, u32[]{:S(2)}) collective-permute-start(bf16[288,1792]{1,0:T(8,128)(2,1)S(1)} %convolution_convert_fusion.2), channel_id=1, source_target_pairs={{0,3},{1,0},{2,1},{3,2},{4,7},{5,4},{6,5},{7,6},{8,11},{9,8},{10,9... | collective-permute-start | bytes 3096584 | tf_op jit(solution)/shard_map/ppermute | solution.py:28
  168.5 41.2 %collective-permute-start.45 = (bf16[288,1792]{1,0:T(8,128)(2,1)S(1)}, bf16[288,1792]{1,0:T(8,128)(2,1)S(1)}, u32[]{:S(2)}, u32[]{:S(2)}) collective-permute-start(bf16[288,1792]{1,0:T(8,128)(2,1)S(1)} %convolution_convert_fusion.1), channel_id=1, source_target_pairs={{0,3},{1,0},{2,1},{3,2},{4,7},{5,4},{6,5},{7,6},{8,11},{9,8},{10,9... | collective-permute-start | bytes 3096584 | tf_op jit(solution)/shard_map/ppermute | solution.py:28
  171.0 41.3 %collective-permute-start.43 = (bf16[288,1792]{1,0:T(8,128)(2,1)S(1)}, bf16[288,1792]{1,0:T(8,128)(2,1)S(1)}, u32[]{:S(2)}, u32[]{:S(2)}) collective-permute-start(bf16[288,1792]{1,0:T(8,128)(2,1)S(1)} %convolution_convert_fusion.3), channel_id=1, source_target_pairs={{0,1},{1,2},{2,3},{3,0},{4,5},{5,6},{6,7},{7,4},{8,9},{9,10},{10,1... | collective-permute-start | bytes 3096584 | tf_op jit(solution)/shard_map/ppermute | solution.py:28
  175.4 80.5 %collective-permute-start.55 = (bf16[288,1792]{1,0:T(8,128)(2,1)S(1)}, bf16[288,1792]{1,0:T(8,128)(2,1)S(1)}, u32[]{:S(2)}, u32[]{:S(2)}) collective-permute-start(bf16[288,1792]{1,0:T(8,128)(2,1)S(1)} %shard_map.136), channel_id=1, source_target_pairs={{0,1},{1,2},{2,3},{3,0},{4,5},{5,6},{6,7},{7,4},{8,9},{9,10},{10,1... | collective-permute-start | bytes 3096584 | tf_op jit(solution)/shard_map/ppermute | solution.py:28
  188.1 91.5 %collective-permute-start.51 = (bf16[288,1792]{1,0:T(8,128)(2,1)S(1)}, bf16[288,1792]{1,0:T(8,128)(2,1)S(1)}, u32[]{:S(2)}, u32[]{:S(2)}) collective-permute-start(bf16[288,1792]{1,0:T(8,128)(2,1)S(1)} %collective-permute-done.48), channel_id=1, source_target_pairs={{0,3},{1,0},{2,1},{3,2},{4,7},{5,4},{6,5},{7,6},{8,11},{9,8},{10,9... | collective-permute-start | bytes 3096584 | tf_op jit(solution)/shard_map/ppermute | solution.py:28
  209.8 41.9 %collective-permute-start.56 = (bf16[288,896]{1,0:T(8,128)(2,1)S(1)}, bf16[288,896]{1,0:T(8,128)(2,1)S(1)}, u32[]{:S(2)}, u32[]{:S(2)}) collective-permute-start(bf16[288,896]{1,0:T(8,128)(2,1)S(1)} %shard_map.139), channel_id=1, source_target_pairs={{0,1},{1,2},{2,3},{3,0},{4,5},{5,6},{6,7},{7,4},{8,9},{9,10},{10,1... | collective-permute-start | bytes 1548296 | tf_op jit(solution)/shard_map/ppermute | solution.py:28
  212.1 27.3 %collective-permute-start.50 = (bf16[288,896]{1,0:T(8,128)(2,1)S(1)}, bf16[288,896]{1,0:T(8,128)(2,1)S(1)}, u32[]{:S(2)}, u32[]{:S(2)}) collective-permute-start(bf16[288,896]{1,0:T(8,128)(2,1)S(1)} %shard_map.139), channel_id=1, source_target_pairs={{0,3},{1,0},{2,1},{3,2},{4,7},{5,4},{6,5},{7,6},{8,11},{9,8},{10,9... | collective-permute-start | bytes 1548296 | tf_op jit(solution)/shard_map/ppermute | solution.py:28
  212.4 37.7 %collective-permute-start.49 = (bf16[288,896]{1,0:T(8,128)(2,1)S(1)}, bf16[288,896]{1,0:T(8,128)(2,1)S(1)}, u32[]{:S(2)}, u32[]{:S(2)}) collective-permute-start(bf16[288,896]{1,0:T(8,128)(2,1)S(1)} %shard_map.137), channel_id=1, source_target_pairs={{0,3},{1,0},{2,1},{3,2},{4,7},{5,4},{6,5},{7,6},{8,11},{9,8},{10,9... | collective-permute-start | bytes 1548296 | tf_op jit(solution)/shard_map/ppermute | solution.py:28
  239.4 16.0 %collective-permute-start.52 = (bf16[288,896]{1,0:T(8,128)(2,1)S(1)}, bf16[288,896]{1,0:T(8,128)(2,1)S(1)}, u32[]{:S(2)}, u32[]{:S(2)}) collective-permute-start(bf16[288,896]{1,0:T(8,128)(2,1)S(1)} %shard_map.137), channel_id=1, source_target_pairs={{0,1},{1,2},{2,3},{3,0},{4,5},{5,6},{6,7},{7,4},{8,9},{9,10},{10,1... | collective-permute-start | bytes 1548296 | tf_op jit(solution)/shard_map/ppermute | solution.py:28
  250.0 31.1 %collective-permute-start.58 = (bf16[288,1792]{1,0:T(8,128)(2,1)S(1)}, bf16[288,1792]{1,0:T(8,128)(2,1)S(1)}, u32[]{:S(2)}, u32[]{:S(2)}) collective-permute-start(bf16[288,1792]{1,0:T(8,128)(2,1)S(1)} %add_convert_fusion), channel_id=1, source_target_pairs={{0,3},{1,0},{2,1},{3,2},{4,7},{5,4},{6,5},{7,6},{8,11},{9,8},{10,9... | collective-permute-start | bytes 3096584 | tf_op jit(solution)/shard_map/ppermute | solution.py:28
  251.6 29.5 %collective-permute-start.57 = (bf16[288,1792]{1,0:T(8,128)(2,1)S(1)}, bf16[288,1792]{1,0:T(8,128)(2,1)S(1)}, u32[]{:S(2)}, u32[]{:S(2)}) collective-permute-start(bf16[288,1792]{1,0:T(8,128)(2,1)S(1)} %add_convert_fusion.1), channel_id=1, source_target_pairs={{0,1},{1,2},{2,3},{3,0},{4,5},{5,6},{6,7},{7,4},{8,9},{9,10},{10,1... | collective-permute-start | bytes 3096584 | tf_op jit(solution)/shard_map/ppermute | solution.py:28
  256.7 21.4 %collective-permute-start.54 = (bf16[288,896]{1,0:T(8,128)(2,1)S(1)}, bf16[288,896]{1,0:T(8,128)(2,1)S(1)}, u32[]{:S(2)}, u32[]{:S(2)}) collective-permute-start(bf16[288,896]{1,0:T(8,128)(2,1)S(1)} %collective-permute-done.50), channel_id=1, source_target_pairs={{0,3},{1,0},{2,1},{3,2},{4,7},{5,4},{6,5},{7,6},{8,11},{9,8},{10,9... | collective-permute-start | bytes 1548296 | tf_op jit(solution)/shard_map/ppermute | solution.py:28
  257.1 22.0 %collective-permute-start.53 = (bf16[288,896]{1,0:T(8,128)(2,1)S(1)}, bf16[288,896]{1,0:T(8,128)(2,1)S(1)}, u32[]{:S(2)}, u32[]{:S(2)}) collective-permute-start(bf16[288,896]{1,0:T(8,128)(2,1)S(1)} %collective-permute-done.52), channel_id=1, source_target_pairs={{0,1},{1,2},{2,3},{3,0},{4,5},{5,6},{6,7},{7,4},{8,9},{9,10},{10,1... | collective-permute-start | bytes 1548296 | tf_op jit(solution)/shard_map/ppermute | solution.py:28
  288.8 17.0 %collective-permute-start.59 = (bf16[288,1024]{1,0:T(8,128)(2,1)S(1)}, bf16[288,1024]{1,0:T(8,128)(2,1)S(1)}, u32[]{:S(2)}, u32[]{:S(2)}) collective-permute-start(bf16[288,1024]{1,0:T(8,128)(2,1)S(1)} %convolution_convert_fusion.7), channel_id=1, source_target_pairs={{0,1},{1,2},{2,3},{3,0},{4,5},{5,6},{6,7},{7,4},{8,9},{9,10},{10,1... | collective-permute-start | bytes 1769480 | tf_op jit(solution)/shard_map/ppermute | solution.py:28
  292.5 47.2 %collective-permute-start.61 = (bf16[288,1024]{1,0:T(8,128)(2,1)S(1)}, bf16[288,1024]{1,0:T(8,128)(2,1)S(1)}, u32[]{:S(2)}, u32[]{:S(2)}) collective-permute-start(bf16[288,1024]{1,0:T(8,128)(2,1)S(1)} %convolution_convert_fusion.6), channel_id=1, source_target_pairs={{0,3},{1,0},{2,1},{3,2},{4,7},{5,4},{6,5},{7,6},{8,11},{9,8},{10,9... | collective-permute-start | bytes 1769480 | tf_op jit(solution)/shard_map/ppermute | solution.py:28
  292.5 27.7 %collective-permute-start.62 = (bf16[288,1024]{1,0:T(8,128)(2,1)S(1)}, bf16[288,1024]{1,0:T(8,128)(2,1)S(1)}, u32[]{:S(2)}, u32[]{:S(2)}) collective-permute-start(bf16[288,1024]{1,0:T(8,128)(2,1)S(1)} %convolution_convert_fusion.5), channel_id=1, source_target_pairs={{0,3},{1,0},{2,1},{3,2},{4,7},{5,4},{6,5},{7,6},{8,11},{9,8},{10,9... | collective-permute-start | bytes 1769480 | tf_op jit(solution)/shard_map/ppermute | solution.py:28
  295.3 45.8 %collective-permute-start.64 = (bf16[288,1024]{1,0:T(8,128)(2,1)S(1)}, bf16[288,1024]{1,0:T(8,128)(2,1)S(1)}, u32[]{:S(2)}, u32[]{:S(2)}) collective-permute-start(bf16[288,1024]{1,0:T(8,128)(2,1)S(1)} %convolution_convert_fusion.4), channel_id=1, source_target_pairs={{0,1},{1,2},{2,3},{3,0},{4,5},{5,6},{6,7},{7,4},{8,9},{9,10},{10,1... | collective-permute-start | bytes 1769480 | tf_op jit(solution)/shard_map/ppermute | solution.py:28
  299.2 21.4 %collective-permute-start.74 = (bf16[288,768]{1,0:T(8,128)(2,1)S(1)}, bf16[288,768]{1,0:T(8,128)(2,1)S(1)}, u32[]{:S(2)}, u32[]{:S(2)}) collective-permute-start(bf16[288,768]{1,0:T(8,128)(2,1)S(1)} %convolution_convert_fusion.11), channel_id=1, source_target_pairs={{0,1},{1,2},{2,3},{3,0},{4,5},{5,6},{6,7},{7,4},{8,9},{9,10},{10,1... | collective-permute-start | bytes 1327112 | tf_op jit(solution)/shard_map/ppermute | solution.py:28
  305.8 47.5 %collective-permute-start.76 = (bf16[288,768]{1,0:T(8,128)(2,1)S(1)}, bf16[288,768]{1,0:T(8,128)(2,1)S(1)}, u32[]{:S(2)}, u32[]{:S(2)}) collective-permute-start(bf16[288,768]{1,0:T(8,128)(2,1)S(1)} %convolution_convert_fusion.10), channel_id=1, source_target_pairs={{0,3},{1,0},{2,1},{3,2},{4,7},{5,4},{6,5},{7,6},{8,11},{9,8},{10,9... | collective-permute-start | bytes 1327112 | tf_op jit(solution)/shard_map/ppermute | solution.py:28
  320.3 17.0 %collective-permute-start.77 = (bf16[288,768]{1,0:T(8,128)(2,1)S(1)}, bf16[288,768]{1,0:T(8,128)(2,1)S(1)}, u32[]{:S(2)}, u32[]{:S(2)}) collective-permute-start(bf16[288,768]{1,0:T(8,128)(2,1)S(1)} %convolution_convert_fusion.9), channel_id=1, source_target_pairs={{0,3},{1,0},{2,1},{3,2},{4,7},{5,4},{6,5},{7,6},{8,11},{9,8},{10,9... | collective-permute-start | bytes 1327112 | tf_op jit(solution)/shard_map/ppermute | solution.py:28
  320.6 16.9 %collective-permute-start.88 = (bf16[64,3584]{1,0:T(8,128)(2,1)S(1)}, bf16[64,3584]{1,0:T(8,128)(2,1)S(1)}, u32[]{:S(2)}, u32[]{:S(2)}) collective-permute-start(bf16[64,3584]{1,0:T(8,128)(2,1)S(1)} %add_convert_fusion.6), channel_id=1, source_target_pairs={{0,28},{1,29},{2,30},{3,31},{4,24},{5,25},{6,26},{7,27},{8,0},{9,1... | collective-permute-start | bytes 1376264 | tf_op jit(solution)/shard_map/ppermute | solution.py:43
  339.8 17.1 %collective-permute-start.79 = (bf16[288,768]{1,0:T(8,128)(2,1)S(1)}, bf16[288,768]{1,0:T(8,128)(2,1)S(1)}, u32[]{:S(2)}, u32[]{:S(2)}) collective-permute-start(bf16[288,768]{1,0:T(8,128)(2,1)S(1)} %convolution_convert_fusion.8), channel_id=1, source_target_pairs={{0,1},{1,2},{2,3},{3,0},{4,5},{5,6},{6,7},{7,4},{8,9},{9,10},{10,1... | collective-permute-start | bytes 1327112 | tf_op jit(solution)/shard_map/ppermute | solution.py:28
  341.1 15.5 %collective-permute-start.75 = (bf16[288,768]{1,0:T(8,128)(2,1)S(1)}, bf16[288,768]{1,0:T(8,128)(2,1)S(1)}, u32[]{:S(2)}, u32[]{:S(2)}) collective-permute-start(bf16[288,768]{1,0:T(8,128)(2,1)S(1)} %fusion.6), channel_id=1, source_target_pairs={{0,1},{1,2},{2,3},{3,0},{4,5},{5,6},{6,7},{7,4},{8,9},{9,10},{10,1... | collective-permute-start | bytes 1327112 | tf_op jit(solution)/shard_map/ppermute | solution.py:28
  348.7 14.1 %collective-permute-start.90 = (bf16[64,3584]{1,0:T(8,128)(2,1)S(1)}, bf16[64,3584]{1,0:T(8,128)(2,1)S(1)}, u32[]{:S(2)}, u32[]{:S(2)}) collective-permute-start(bf16[64,3584]{1,0:T(8,128)(2,1)S(1)} %add_convert_fusion.5), channel_id=1, source_target_pairs={{0,28},{1,29},{2,30},{3,31},{4,24},{5,25},{6,26},{7,27},{8,0},{9,1... | collective-permute-start | bytes 1376264 | tf_op jit(solution)/shard_map/ppermute | solution.py:43
  353.3 14.7 %collective-permute-start.92 = (bf16[64,3584]{1,0:T(8,128)(2,1)S(1)}, bf16[64,3584]{1,0:T(8,128)(2,1)S(1)}, u32[]{:S(2)}, u32[]{:S(2)}) collective-permute-start(bf16[64,3584]{1,0:T(8,128)(2,1)S(1)} %add_convert_fusion.4), channel_id=1, source_target_pairs={{0,8},{1,9},{2,10},{3,11},{4,12},{5,13},{6,14},{7,15},{8,16},{9,17... | collective-permute-start | bytes 1376264 | tf_op jit(solution)/shard_map/ppermute | solution.py:43
  356.6 14.4 %collective-permute-start.65 = (bf16[64,2048]{1,0:T(8,128)(2,1)S(1)}, bf16[64,2048]{1,0:T(8,128)(2,1)S(1)}, u32[]{:S(2)}, u32[]{:S(2)}) collective-permute-start(bf16[64,2048]{1,0:T(8,128)(2,1)S(1)} %get-tuple-element.125), channel_id=1, source_target_pairs={{0,8},{1,9},{2,10},{3,11},{4,12},{5,13},{6,14},{7,15},{8,16},{9,17... | collective-permute-start | bytes 786440 | tf_op jit(solution)/shard_map/ppermute | solution.py:43
  356.9 14.5 %collective-permute-start.69 = (bf16[64,2048]{1,0:T(8,128)(2,1)S(1)}, bf16[64,2048]{1,0:T(8,128)(2,1)S(1)}, u32[]{:S(2)}, u32[]{:S(2)}) collective-permute-start(bf16[64,2048]{1,0:T(8,128)(2,1)S(1)} %get-tuple-element.128), channel_id=1, source_target_pairs={{0,28},{1,29},{2,30},{3,31},{4,24},{5,25},{6,26},{7,27},{8,0},{9,1... | collective-permute-start | bytes 786440 | tf_op jit(solution)/shard_map/ppermute | solution.py:43
  368.0 26.8 %collective-permute-start.91 = (bf16[64,3584]{1,0:T(8,128)(2,1)S(1)}, bf16[64,3584]{1,0:T(8,128)(2,1)S(1)}, u32[]{:S(2)}, u32[]{:S(2)}) collective-permute-start(bf16[64,3584]{1,0:T(8,128)(2,1)S(1)} %add_convert_fusion.3), channel_id=1, source_target_pairs={{0,28},{1,29},{2,30},{3,31},{4,24},{5,25},{6,26},{7,27},{8,0},{9,1... | collective-permute-start | bytes 1376264 | tf_op jit(solution)/shard_map/ppermute | solution.py:43
  371.1 25.9 %collective-permute-start.93 = (bf16[64,3584]{1,0:T(8,128)(2,1)S(1)}, bf16[64,3584]{1,0:T(8,128)(2,1)S(1)}, u32[]{:S(2)}, u32[]{:S(2)}) collective-permute-start(bf16[64,3584]{1,0:T(8,128)(2,1)S(1)} %add_convert_fusion.2), channel_id=1, source_target_pairs={{0,8},{1,9},{2,10},{3,11},{4,12},{5,13},{6,14},{7,15},{8,16},{9,17... | collective-permute-start | bytes 1376264 | tf_op jit(solution)/shard_map/ppermute | solution.py:43
  371.4 16.5 %collective-permute-start.66 = (bf16[64,2048]{1,0:T(8,128)(2,1)S(1)}, bf16[64,2048]{1,0:T(8,128)(2,1)S(1)}, u32[]{:S(2)}, u32[]{:S(2)}) collective-permute-start(bf16[64,2048]{1,0:T(8,128)(2,1)S(1)} %add_convert_fusion.12), channel_id=1, source_target_pairs={{0,8},{1,9},{2,10},{3,11},{4,12},{5,13},{6,14},{7,15},{8,16},{9,17... | collective-permute-start | bytes 786440 | tf_op jit(solution)/shard_map/ppermute | solution.py:43
  371.6 16.4 %collective-permute-start.70 = (bf16[64,2048]{1,0:T(8,128)(2,1)S(1)}, bf16[64,2048]{1,0:T(8,128)(2,1)S(1)}, u32[]{:S(2)}, u32[]{:S(2)}) collective-permute-start(bf16[64,2048]{1,0:T(8,128)(2,1)S(1)} %add_convert_fusion.9), channel_id=1, source_target_pairs={{0,28},{1,29},{2,30},{3,31},{4,24},{5,25},{6,26},{7,27},{8,0},{9,1... | collective-permute-start | bytes 786440 | tf_op jit(solution)/shard_map/ppermute | solution.py:43
  388.2 13.6 %collective-permute-start.71 = (bf16[64,2048]{1,0:T(8,128)(2,1)S(1)}, bf16[64,2048]{1,0:T(8,128)(2,1)S(1)}, u32[]{:S(2)}, u32[]{:S(2)}) collective-permute-start(bf16[64,2048]{1,0:T(8,128)(2,1)S(1)} %add_convert_fusion.8), channel_id=1, source_target_pairs={{0,28},{1,29},{2,30},{3,31},{4,24},{5,25},{6,26},{7,27},{8,0},{9,1... | collective-permute-start | bytes 786440 | tf_op jit(solution)/shard_map/ppermute | solution.py:43
  394.9 13.3 %collective-permute-start.86 = (bf16[64,1536]{1,0:T(8,128)(2,1)S(1)}, bf16[64,1536]{1,0:T(8,128)(2,1)S(1)}, u32[]{:S(2)}, u32[]{:S(2)}) collective-permute-start(bf16[64,1536]{1,0:T(8,128)(2,1)S(1)} %add_convert_fusion.14), channel_id=1, source_target_pairs={{0,8},{1,9},{2,10},{3,11},{4,12},{5,13},{6,14},{7,15},{8,16},{9,17... | collective-permute-start | bytes 589832 | tf_op jit(solution)/shard_map/ppermute | solution.py:43
  (76 other events, 774.3 us)
